TPU v7x, 512 devices: a whole 4x8x8 slice. The times are simulated.
512 devices in a mesh: dp: 32 (over y, x_hi, core), tensor: 16 (over x_lo, z).
Axes of the slice: x: 4 (x_hi: 2, x_lo: 2; x = x_hi * 2 + x_lo), y: 8, z: 8, core: 2. Of those that a mesh axis runs over, the one named last changes fastest.
Arguments:
- master: float32 [512, 53248], P('dp', 'tensor')
- checks: bfloat16 [512, 64], P('dp', 'tensor'), may hold values from -6 to 6
Outputs:
- quantized: bfloat16 [512, 53248], P(None, 'tensor')
- block_scales: float32 [4, 416], P(None, 'tensor')
- probe_out: float32 [64, 53248], P(None, 'tensor')
All inputs are finite; a program needn't handle non-finite values. Where the computation divides by a largest or mean magnitude, that divisor is 1e-20 or more.
Results may differ from a plain program's by a relative error of at most 0.0051.
Values may be sent and summed in bfloat16 or wider, within the bound.
No kernel may reach another device: no remote copies, remote signals or barrier semaphores. Data moves between devices by JAX's collectives and lax.ppermute only.
A program may use at most 64 MiB of HBM per device.

v0:
```python
import jax
import jax.numpy as jnp
from jax import lax
from jax.sharding import PartitionSpec as P

BLOCK = 128


epsilon = 1e-06


def contract_rows(left, right):
    return lax.dot_general(
        left, right, (((0,), (0,)), ((), ())), preferred_element_type=jnp.float32
    )


def per_device(master, checks):
    row_dev = master.shape[0]
    col_dev = master.shape[1]
    all_rows = row_dev * lax.axis_size("dp")
    n_row_blocks = all_rows // BLOCK
    n_col_blocks = col_dev // BLOCK
    check_cols = lax.all_gather(checks, "tensor", axis=1, tiled=True)
    gathered, check_all = (
        lax.all_gather(master, "dp", axis=0, tiled=True),
        lax.all_gather(check_cols.astype(jnp.float32), "dp", axis=0, tiled=True).astype(
            check_cols.dtype
        ),
    )
    tiles = gathered.reshape(n_row_blocks, BLOCK, n_col_blocks, BLOCK)
    scales = jnp.max(jnp.abs(tiles), axis=(1, 3)) + epsilon
    codes = (tiles / scales[:, None, :, None]).reshape(all_rows, col_dev).astype(jnp.bfloat16)
    restored = (
        (codes.astype(jnp.float32).reshape(tiles.shape) * scales[:, None, :, None])
        .reshape(all_rows, col_dev)
        .astype(jnp.bfloat16)
    )
    probes = contract_rows(check_all, restored)
    return (codes, scales, probes)


def solution(mesh):
    return jax.shard_map(
        per_device,
        mesh=mesh,
        in_specs=(P("dp", "tensor"), P("dp", "tensor")),
        out_specs=(P(None, "tensor"), P(None, "tensor"), P(None, "tensor")),
        check_vma=False,
    )
```

profile of v0, /device:TPU:1, one launch (start us, length us, event | category | flops | bytes accessed | tf_op | source)
XLA Modules:
  0.0 177.4 jit_solution(11057529068375055361)
XLA Ops:
  7.2 0.0 all-gather.3.cloned.1.call-start
  7.2 0.7 all-gather.3.cloned.1.call-update
  7.9 33.6 %all-gather = bf16[16,4,16]{2,1,0:T(4,128)(2,1)S(1)} all-gather(bf16[1,4,16]{2,1,0:T(4,128)(2,1)} %bitcast.27), channel_id=1, replica_groups=mesh['dp'=32,'tensor'=16] {'tensor'}, dimensions={0}, use_global_device_ids=true | all-gather | bytes 2176 | tf_op jit(solution)/shard_map/all_gather | solution.py:24
  41.5 0.1 copy.10
  41.6 50.2 %all_gather.11 = bf16[512,64]{1,0:T(8,128)(2,1)S(1)} all-gather(bf16[16,64]{1,0:T(8,128)(2,1)S(1)} %bitcast.26), channel_id=1, replica_groups=mesh['dp'=32,'tensor'=16] {'dp'}, dimensions={0}, use_global_device_ids=true | all-gather | bytes 67584 | tf_op jit(solution)/shard_map/all_gather | solution.py:27
  91.8 27.4 %all-gather.3.cloned.1.call-done = f32[512,3328]{1,0:T(8,128)} async-done(((f32[16,3328]{1,0:T(8,128)}), f32[512,3328]{1,0:T(8,128)}) %all-gather.3.cloned.1.call-update) | async-done | bytes 6815760 | tf_op jit(solution)/shard_map/all_gather | solution.py:26
  119.2 6.2 %abs.6 = f32[512,3328]{1,0:T(8,128)} abs(f32[512,3328]{1,0:T(8,128)} %all-gather.3.cloned.1.call-done) | non-fusion elementwise | flops 1703936 | bytes 13631488 | tf_op jit(solution)/shard_map/abs | solution.py:32
  125.5 7.6 %copy.8 = f32[512,3328]{0,1:T(8,128)} copy(f32[512,3328]{1,0:T(8,128)} %abs.6) | data formatting | bytes 13631488 | tf_op jit(solution)/shard_map/abs | solution.py:32
  133.1 8.6 %abs.7 = f32[4,128,26,128]{1,0,3,2:T(4,128)} reshape(f32[512,3328]{0,1:T(8,128)} %copy.8) | data formatting | bytes 13631488 | tf_op jit(solution)/shard_map/abs | solution.py:32
  141.7 4.0 %reduce_max.9 = f32[4,26]{0,1:T(8,128)S(1)} reduce(f32[4,128,26,128]{1,0,3,2:T(4,128)} %abs.7, f32[]{:T(128)} %constant.0.clone.1), dimensions={1,3}, to_apply=%region_0.0 | reduce | flops 1703832 | bytes 6816164 | tf_op jit(solution)/shard_map/reduce_max | solution.py:32
  145.7 0.7 copy.12
  146.4 7.6 %copy.9 = f32[512,3328]{0,1:T(8,128)} copy(f32[512,3328]{1,0:T(8,128)} %all-gather.3.cloned.1.call-done) | data formatting | bytes 13631488 | tf_op jit(solution)/shard_map/all_gather | solution.py:26
  154.0 0.9 div.11
  154.9 0.0 copy-start
  155.0 2.8 %copy-done = f32[4,128,26,128]{1,0,3,2:T(4,128)} copy-done((f32[4,128,26,128]{1,0,3,2:T(4,128)}, f32[4,128,26,128]{1,0,3,2:T(4,128)S(1)}, u32[]{:S(2)}) %copy-start) | copy-done | bytes 6815768
  157.7 4.3 %fusion = bf16[512,3328]{0,1:T(8,128)(2,1)S(1)} fusion(f32[512,3328]{0,1:T(8,128)} %copy.9, f32[416,8,4,128]{3,2,1,0:T(4,128)S(1)} %bitcast.23), kind=kLoop, calls=%fused_computation.2 | loop fusion | flops 3407872 | bytes 17039360 | tf_op jit(solution)/shard_map/convert_element_type | solution.py:33
  162.1 3.5 %copy.11 = bf16[512,3328]{1,0:T(8,128)(2,1)} copy(bf16[512,3328]{0,1:T(8,128)(2,1)S(1)} %fusion) | data formatting | bytes 6815744
  165.6 5.0 %convolution_bitcast_fusion = f32[64,3328]{1,0:T(8,128)} fusion(bf16[512,3328]{0,1:T(8,128)(2,1)S(1)} %fusion, f32[416,8,4,128]{3,2,1,0:T(4,128)} %bitcast.24, bf16[512,64]{1,0:T(8,128)(2,1)S(1)} %all_gather.11), kind=kOutput, calls=%fused_computation.4 | convolution fusion | flops 223215616 | bytes 11141120 | tf_op jit(solution)/shard_map/dot_general | solution.py:13
  (1 shorter events, 0.0 us)
Async XLA Ops:
  7.2 112.0 %all-gather.3.cloned.1.call-start = ((), (), s32[]{:S(2)}) async-start(), calls=%async_computation | async-start | bytes 7028736 | tf_op jit(solution)/shard_map/all_gather | solution.py:26
  154.9 2.8 %copy-start = (f32[4,128,26,128]{1,0,3,2:T(4,128)}, f32[4,128,26,128]{1,0,3,2:T(4,128)S(1)}, u32[]{:S(2)}) copy-start(f32[4,128,26,128]{1,0,3,2:T(4,128)S(1)} %div.11) | copy-start | bytes 20447236
Sparse Core Ops, SparseCore 0:
  11.3 107.8 all-gather.2
where the time goes:
time: 178 us; the launch traced here: 177 us
  blocking collectives  83.8 us (47%)
  local copies, waits for them, and re-layouts  31.9 us (18%)
  waiting for transfers between devices  28.1 us (16%)
  other arithmetic  14.5 us (8%)
  between operations  14.1 us (8%)
  matrix products  5 us (3%)
    all_gather x1, blocking collectives, per_device(): lax.all_gather(check_cols.astype(jnp.float32), 'dp', axis=0, tiled=True)  50.2 us
    all_gather x1, blocking collectives, per_device(): check_cols = lax.all_gather(checks, 'tensor', axis=1, tiled=True)  33.6 us
    all_gather x1, waiting for transfers between devices, per_device(): lax.all_gather(master, 'dp', axis=0, tiled=True)  27.4 us
    abs x2, local copies, waits for them, and re-layouts, per_device(): scales = jnp.max(jnp.abs(tiles), axis=(1, 3)) + epsilon  16.3 us
    all_gather x1, local copies, waits for them, and re-layouts, per_device(): lax.all_gather(master, 'dp', axis=0, tiled=True)  7.64 us
    unnamed x4, local copies, waits for them, and re-layouts  6.94 us
    abs x1, other arithmetic, per_device(): scales = jnp.max(jnp.abs(tiles), axis=(1, 3)) + epsilon  6.24 us
    dot_general x1, matrix products, contract_rows(): lax.dot_general(left, right, (((0,), (0,)), ((), ())), preferred_element_...  5 us
  transfers between devices with their start and end apart: 1, of which 1 were waited for; matrix products, arithmetic and copies ran while one was open for 0% of the time, Pallas kernels for 0%

commit v1 on v0

v1 whole, which is shorter than its diff:
```python
import functools

import jax
import jax.numpy as jnp
import numpy as np
from jax import lax
from jax.experimental import pallas as pl
from jax.experimental.pallas import tpu as pltpu
from jax.sharding import PartitionSpec as P

BLOCK = 128
EPS = 1e-06
Y = 8
LANES = 128
HALF = 64
TILE = 256

CORES = [[2 * i, 2 * i + 1] for i in range(16)]


def along_y(step):
    pairs = []
    for y in range(Y):
        for rest in range(4):
            to = (y + step if rest % 2 == 0 else y - step) % Y
            pairs.append((y * 4 + rest, to * 4 + rest))
    return pairs


ACROSS_X = [(i, i ^ 2) for i in range(32)]


def both_cores(a):
    return lax.all_gather(a, "dp", axis_index_groups=CORES, axis=0, tiled=True)


def prepare_kernel(m_ref, x_ref, part_ref):
    m = m_ref[...]
    x_ref[...] = m.astype(jnp.bfloat16)
    high = jnp.max(jnp.abs(m), axis=0, keepdims=True)
    lane = lax.broadcasted_iota(jnp.int32, (1, HALF), 1)
    tops = jnp.zeros((1, HALF), jnp.float32)
    for j in range(m.shape[1] // BLOCK):
        top = jnp.max(high[:, j * BLOCK : (j + 1) * BLOCK], axis=1, keepdims=True)
        tops = jnp.where(lane == j, top, tops)
    first = tops.astype(jnp.bfloat16).astype(jnp.float32)
    second = (tops - first).astype(jnp.bfloat16).astype(jnp.float32)
    third = tops - first - second
    row = lax.broadcasted_iota(jnp.int32, (16, HALF), 0)
    part = jnp.where(row == 0, first, jnp.where(row == 1, second, third))
    part_ref[...] = jnp.where(row < 3, part, 0.0).astype(jnp.bfloat16)


def prepare(m):
    rows, cols = m.shape
    return pl.pallas_call(
        prepare_kernel,
        out_shape=(
            jax.ShapeDtypeStruct((rows, cols), jnp.bfloat16),
            jax.ShapeDtypeStruct((rows, HALF), jnp.bfloat16),
        ),
        name="prepare",
    )(m)


def pieces():
    out = [("own", 0, 0, 0), ("own", 32, 0, 1)]
    for core, sign in ((0, -1), (1, 1)):
        for name, place in (("two", 2), ("one", 1), ("three", 3)):
            for part in (0, 1):
                out.append((name, core * 64 + part * 32, sign * place, part))
        out.append(("four", core * 32, 4, core))
    return out


def export_kernel(at_ref, tab_ref, own_ref, two_ref, one_ref, three_ref, four_ref, codes_ref, scales_ref, probe_ref, scale_s, inv_s, checks_s):
    n_blocks = scales_ref.shape[1]
    tile = codes_ref.shape[1]

    @pl.when(pl.program_id(0) == 0)
    def _():
        tab = tab_ref[...].astype(jnp.float32)
        checks_s[...] = tab.T[HALF:, :].astype(jnp.bfloat16)
        terms = tab.reshape(32, 16, LANES)
        tops = terms[:, 0, :] + terms[:, 1, :] + terms[:, 2, :]
        scale = jnp.max(tops.reshape(4, 8, LANES), axis=1) + EPS
        scales_ref[...] = scale[:, :n_blocks]
        inv = 1.0 / scale
        for j in range(n_blocks):
            cols = slice(j * BLOCK, (j + 1) * BLOCK)
            scale_s[:, cols] = jnp.broadcast_to(scale[:, j : j + 1], (4, BLOCK))
            inv_s[:, cols] = jnp.broadcast_to(inv[:, j : j + 1], (4, BLOCK))

    refs = dict(own=own_ref, two=two_ref, one=one_ref, three=three_ref, four=four_ref)
    y, xh = at_ref[0], at_ref[1]
    start = pl.multiple_of(pl.program_id(0) * tile, BLOCK)
    for name, row, place, part in pieces():
        to = lax.rem(y + place + Y, Y)
        side = xh if part == 0 else 1 - xh
        inv = inv_s[pl.ds(to // 2, 1), pl.ds(start, tile)]
        value = refs[name][row : row + 32, :].astype(jnp.float32) * inv
        dest = pl.multiple_of(to * 64 + side * 32, 32)
        codes_ref[pl.ds(dest, 32), :] = value.astype(jnp.bfloat16)
    total = jnp.zeros(probe_ref.shape, jnp.float32)
    for g in range(4):
        part = jnp.dot(
            checks_s[:, g * BLOCK : (g + 1) * BLOCK],
            codes_ref[g * BLOCK : (g + 1) * BLOCK, :],
            preferred_element_type=jnp.float32,
        )
        total = total + part * scale_s[g : g + 1, pl.ds(start, tile)]
    probe_ref[...] = total


def export(at, tab, *received):
    cols = received[0].shape[1]
    whole = lambda a: pl.BlockSpec(a.shape, lambda i: (0, 0))
    strip = lambda a: pl.BlockSpec((a.shape[0], TILE), lambda i: (0, i))
    return pl.pallas_call(
        export_kernel,
        grid=(cols // TILE,),
        in_specs=[
            pl.BlockSpec(memory_space=pltpu.SMEM),
            whole(tab),
            *map(strip, received),
        ],
        out_specs=(
            pl.BlockSpec((512, TILE), lambda i: (0, i)),
            pl.BlockSpec((4, cols // BLOCK), lambda i: (0, 0)),
            pl.BlockSpec((64, TILE), lambda i: (0, i)),
        ),
        out_shape=(
            jax.ShapeDtypeStruct((512, cols), jnp.bfloat16),
            jax.ShapeDtypeStruct((4, cols // BLOCK), jnp.float32),
            jax.ShapeDtypeStruct((64, cols), jnp.float32),
        ),
        scratch_shapes=[
            pltpu.VMEM((4, cols), jnp.float32),
            pltpu.VMEM((4, cols), jnp.float32),
            pltpu.VMEM((64, 512), jnp.bfloat16),
        ],
        compiler_params=pltpu.CompilerParams(vmem_limit_bytes=24 * 1024 * 1024),
        name="export",
    )(at, tab, *received)


def after(a, *others):
    return lax.optimization_barrier((a, *others))[0]


def per_device(master, checks):
    me = lax.axis_index("dp")
    core = me % 2
    at = jnp.stack([me // 4, (me // 2) % 2]).astype(jnp.int32)
    x, part = prepare(master)
    other = lax.ppermute(x, "dp", ACROSS_X)
    a = both_cores(x)
    two_a = lax.ppermute(a, "dp", along_y(2))
    b = both_cores(other)
    two_b = lax.ppermute(b, "dp", along_y(2))
    own = jnp.concatenate([a, b], 0)
    one = lax.ppermute(own, "dp", along_y(1))
    sent = after(checks, b)
    spread = lax.all_to_all(jnp.broadcast_to(sent[None], (16, 16, 4)), "tensor", 0, 0)
    rows = spread.transpose(1, 0, 2).reshape(16, HALF)
    two = jnp.concatenate([two_a, two_b], 0)
    three = lax.ppermute(two, "dp", along_y(1))
    four = lax.ppermute(jnp.where(core == 0, two_a, two_b), "dp", along_y(2))
    two = both_cores(after(two, one))
    one = both_cores(one)
    table = after(jnp.concatenate([part, rows], 1), one)
    tab = lax.all_to_all(jnp.broadcast_to(table[None], (32, 16, LANES)), "dp", 0, 0)
    three, four = both_cores(three), both_cores(four)
    codes, scales, probes = export(at, tab.reshape(512, LANES), own, two, one, three, four)
    return codes, scales, probes


def solution(mesh):
    return jax.shard_map(
        per_device,
        mesh=mesh,
        in_specs=(P("dp", "tensor"), P("dp", "tensor")),
        out_specs=(P(None, "tensor"), P(None, "tensor"), P(None, "tensor")),
        check_vma=False,
    )
```

time: 178 us -> 79.2 us (0.44)
  blocking collectives: 83.8 us -> 17.5 us
  starting transfers between devices: 0.04 us -> 38.7 us
  local copies, waits for them, and re-layouts: 31.9 us -> 2.08 us
  waiting for transfers between devices: 28.1 us -> 8.87 us
  between operations: 14.1 us -> 0.8 us
  other arithmetic: 14.5 us -> 1.59 us
  Pallas kernels: 0 us -> 9.13 us
  matrix products: 5 us -> 0 us
    all_gather x2 -> x6, blocking collectives: 83.8 us -> 17.5 us  [both_cores(): return lax.all_gather(a, 'dp', axis_index_groups=CORES, axis=0, tiled=True)]
    all_gather x1 -> x0, waiting for transfers between devices: 27.4 us -> none  [per_device(): lax.all_gather(master, 'dp', axis=0, tiled=True)]
    ppermute x0 -> x6, starting transfers between devices: none -> 21.5 us  [the longest x1 5.47 us: per_device(): other = lax.ppermute(x, 'dp', ACROSS_X)]
    all_to_all x0 -> x2, starting transfers between devices: none -> 17.2 us  [the longest x1 9.78 us: per_device(): lax.all_to_all(jnp.broadcast_to(sent[None], (16, 16, 4)), 'tensor', 0, 0)]
    abs x2 -> x0, local copies, waits for them, and re-layouts: 16.3 us -> none  [per_device(): scales = jnp.max(jnp.abs(tiles), axis=(1, 3)) + epsilon]
    pallas_call x0 -> x2, Pallas kernels: none -> 9.13 us  [the longest x1 7.48 us: export(): pl.pallas_call(export_kernel, grid=(cols // TILE,), in_specs=[pl.BlockSpe...]
    all_to_all x0 -> x2, waiting for transfers between devices: none -> 8.85 us  [the longest x1 5.22 us: per_device(): lax.all_to_all(jnp.broadcast_to(sent[None], (16, 16, 4)), 'tensor', 0, 0)]
    all_gather x1 -> x0, local copies, waits for them, and re-layouts: 7.64 us -> none  [per_device(): lax.all_gather(master, 'dp', axis=0, tiled=True)]
  transfers between devices with their start and end apart: 1 -> 8, of which waited for: 1 -> 2; matrix products, arithmetic and copies ran while one was open for 0% -> 5% of each run, Pallas kernels for 0% -> 0%
where the time goes in v1:
time: 79.2 us; the launch traced here: 78.7 us
  starting transfers between devices  38.7 us (49%)
  blocking collectives  17.5 us (22%)
  Pallas kernels  9.13 us (12%)
  waiting for transfers between devices  8.87 us (11%)
  local copies, waits for them, and re-layouts  2.08 us (3%)
  other arithmetic  1.59 us (2%)
  between operations  0.8 us (1%)
    all_gather x6, blocking collectives, both_cores(): return lax.all_gather(a, 'dp', axis_index_groups=CORES, axis=0, tiled=True)  17.5 us
    all_to_all x1, starting transfers between devices, per_device(): lax.all_to_all(jnp.broadcast_to(sent[None], (16, 16, 4)), 'tensor', 0, 0)  9.78 us
    pallas_call x1, Pallas kernels, export(): pl.pallas_call(export_kernel, grid=(cols // TILE,), in_specs=[pl.BlockSpe...  7.48 us
    all_to_all x1, starting transfers between devices, per_device(): lax.all_to_all(jnp.broadcast_to(table[None], (32, 16, LANES)), 'dp', 0, 0)  7.38 us
    ppermute x1, starting transfers between devices, per_device(): other = lax.ppermute(x, 'dp', ACROSS_X)  5.47 us
    all_to_all x1, waiting for transfers between devices, per_device(): lax.all_to_all(jnp.broadcast_to(sent[None], (16, 16, 4)), 'tensor', 0, 0)  5.22 us
    ppermute x1, starting transfers between devices, per_device(): three = lax.ppermute(two, 'dp', along_y(1))  4.19 us
    all_to_all x1, waiting for transfers between devices, per_device(): lax.all_to_all(jnp.broadcast_to(table[None], (32, 16, LANES)), 'dp', 0, 0)  3.63 us
  transfers between devices with their start and end apart: 8, of which 2 were waited for; matrix products, arithmetic and copies ran while one was open for 5% of the time, Pallas kernels for 0%

profile of v1, /device:TPU:1, one launch (start us, length us, event | category | flops | bytes accessed | tf_op | source)
XLA Modules:
  0.0 78.7 jit_solution(7617525259819368264)
XLA Ops:
  0.6 1.6 %prepare.1 = (bf16[16,3328]{1,0:T(8,128)(2,1)}, bf16[16,64]{1,0:T(8,128)(2,1)}) custom-call(f32[16,3328]{1,0:T(8,128)} %m_ref.1), custom_call_target="tpu_custom_call" | custom-call | tf_op jit(solution)/shard_map/prepare/pallas_call | solution.py:56
  2.3 5.5 %collective-permute-start = (bf16[16,3328]{1,0:T(8,128)(2,1)}, bf16[16,3328]{1,0:T(8,128)(2,1)S(1)}, u32[]{:S(2)}, u32[]{:S(2)}) collective-permute-start(bf16[16,3328]{1,0:T(8,128)(2,1)} %get-tuple-element.9), channel_id=1, source_target_pairs={{0,32},{16,48},{32,0},{48,16},{64,96},{80,112},{96,64},{112,80},{1... | collective-permute-start | bytes 319496 | tf_op jit(solution)/shard_map/ppermute | solution.py:156
  7.8 5.1 %all_gather.19 = bf16[32,3328]{1,0:T(8,128)(2,1)S(1)} all-gather(bf16[16,3328]{1,0:T(8,128)(2,1)} %get-tuple-element.9), channel_id=1, replica_groups={{0,16},{32,48},{64,80},{96,112},{128,144},{160,176},{192,208},{224,240}..., dimensions={0}, use_global_device_ids=true | all-gather | bytes 319488 | tf_op jit(solution)/shard_map/all_gather | solution.py:34
  12.9 3.5 %collective-permute-start.2 = (bf16[32,3328]{1,0:T(8,128)(2,1)S(1)}, bf16[32,3328]{1,0:T(8,128)(2,1)S(1)}, u32[]{:S(2)}, u32[]{:S(2)}) collective-permute-start(bf16[32,3328]{1,0:T(8,128)(2,1)S(1)} %all_gather.19), channel_id=1, source_target_pairs={{0,128},{16,400},{32,160},{48,432},{64,192},{80,464},{96,224},{112... | collective-permute-start | bytes 638984 | tf_op jit(solution)/shard_map/ppermute | solution.py:158
  16.5 0.1 pad_add_fusion.at_ref
  16.6 0.0 collective-permute-done
  16.6 2.5 %all_gather.18 = bf16[32,3328]{1,0:T(8,128)(2,1)S(1)} all-gather(bf16[16,3328]{1,0:T(8,128)(2,1)S(1)} %collective-permute-done), channel_id=1, replica_groups={{0,16},{32,48},{64,80},{96,112},{128,144},{160,176},{192,208},{224,240}..., dimensions={0}, use_global_device_ids=true | all-gather | bytes 319488 | tf_op jit(solution)/shard_map/all_gather | solution.py:34
  19.0 3.6 %collective-permute-start.3 = (bf16[32,3328]{1,0:T(8,128)(2,1)S(1)}, bf16[32,3328]{1,0:T(8,128)(2,1)S(1)}, u32[]{:S(2)}, u32[]{:S(2)}) collective-permute-start(bf16[32,3328]{1,0:T(8,128)(2,1)S(1)} %all_gather.18), channel_id=1, source_target_pairs={{0,128},{16,400},{32,160},{48,432},{64,192},{80,464},{96,224},{112... | collective-permute-start | bytes 638984 | tf_op jit(solution)/shard_map/ppermute | solution.py:160
  22.7 1.3 %broadcast_in_dim.4 = bf16[16,16,4]{1,2,0:T(4,128)(2,1)} broadcast(bf16[16,4]{0,1:T(4,128)(2,1)} %param.3), dimensions={1,2} | broadcast | bytes 2176 | tf_op jit(solution)/shard_map/broadcast_in_dim | solution.py:164
  24.0 9.8 %all-to-all-start = ((bf16[16,16,4]{1,2,0:T(4,128)(2,1)}), bf16[16,16,4]{1,2,0:T(4,128)(2,1)S(1)}, u32[]{:S(2)}, u32[]{:S(2)}) async-start(bf16[16,16,4]{1,2,0:T(4,128)(2,1)} %broadcast_in_dim.4), calls=%async_computation | async-start | bytes 32768 | tf_op jit(solution)/shard_map/all_to_all | solution.py:164
  33.8 2.1 %collective-permute-start.1 = (bf16[64,3328]{1,0:T(8,128)(2,1)S(1)}, bf16[64,3328]{1,0:T(8,128)(2,1)S(1)}, u32[]{:S(2)}, u32[]{:S(2)}) collective-permute-start(bf16[64,3328]{1,0:T(8,128)(2,1)S(1)} %constant_dynamic-update-slice_fusion.own_ref), channel_id=1, source_target_pairs={{0,64},{16,464},{32,96},{48,496},{64,128},{80,16},{96,160},{112,48... | collective-permute-start | bytes 1277960 | tf_op jit(solution)/shard_map/ppermute | solution.py:162
  35.9 5.2 %all-to-all-done = bf16[16,16,4]{1,2,0:T(4,128)(2,1)S(1)} async-done(((bf16[16,16,4]{1,2,0:T(4,128)(2,1)}), bf16[16,16,4]{1,2,0:T(4,128)(2,1)S(1)}, u32[]{:S(2)}, u32[]{:S(2)}) %all-to-all-start) | async-done | bytes 2080 | tf_op jit(solution)/shard_map/all_to_all | solution.py:164
  41.1 0.1 copy.6
  41.1 0.8 pad_maximum_fusion
  41.9 0.0 collective-permute-done.2
  41.9 0.0 collective-permute-done.3
  42.0 0.7 broadcast_select_fusion
  42.7 2.7 %collective-permute-start.5 = (bf16[32,3328]{1,0:T(8,128)(2,1)}, bf16[32,3328]{1,0:T(8,128)(2,1)S(1)}, u32[]{:S(2)}, u32[]{:S(2)}) collective-permute-start(bf16[32,3328]{1,0:T(8,128)(2,1)} %get-tuple-element.13), channel_id=1, source_target_pairs={{0,128},{16,400},{32,160},{48,432},{64,192},{80,464},{96,224},{112... | collective-permute-start | bytes 638984 | tf_op jit(solution)/shard_map/ppermute | solution.py:168
  45.4 4.2 %collective-permute-start.4 = (bf16[64,3328]{1,0:T(8,128)(2,1)S(1)}, bf16[64,3328]{1,0:T(8,128)(2,1)}, u32[]{:S(2)}, u32[]{:S(2)}) collective-permute-start(bf16[64,3328]{1,0:T(8,128)(2,1)S(1)} %get-tuple-element.12), channel_id=1, source_target_pairs={{0,64},{16,464},{32,96},{48,496},{64,128},{80,16},{96,160},{112,48... | collective-permute-start | bytes 1277960 | tf_op jit(solution)/shard_map/ppermute | solution.py:167
  49.6 0.0 collective-permute-done.1
  49.6 2.8 %all_gather.20.one_ref = bf16[128,3328]{1,0:T(8,128)(2,1)S(1)} all-gather(bf16[64,3328]{1,0:T(8,128)(2,1)S(1)} %collective-permute-done.1), channel_id=1, replica_groups={{0,16},{32,48},{64,80},{96,112},{128,144},{160,176},{192,208},{224,240}..., dimensions={0}, use_global_device_ids=true | all-gather | bytes 1277952 | tf_op jit(solution)/shard_map/all_gather | solution.py:34
  52.4 0.7 broadcast_in_dim.5
  53.1 7.4 %all-to-all-start.1 = ((bf16[32,16,128]{2,1,0:T(8,128)(2,1)}), bf16[32,16,128]{2,1,0:T(8,128)(2,1)S(1)}, u32[]{:S(2)}, u32[]{:S(2)}) async-start(bf16[32,16,128]{2,1,0:T(8,128)(2,1)} %broadcast_in_dim.5), calls=%async_computation.1 | async-start | bytes 262144 | tf_op jit(solution)/shard_map/all_to_all | solution.py:172
  60.4 2.4 %all_gather.21.two_ref = bf16[128,3328]{1,0:T(8,128)(2,1)S(1)} all-gather(bf16[64,3328]{1,0:T(8,128)(2,1)S(1)} %get-tuple-element.12), channel_id=1, replica_groups={{0,16},{32,48},{64,80},{96,112},{128,144},{160,176},{192,208},{224,240}..., dimensions={0}, use_global_device_ids=true | all-gather | bytes 1277952 | tf_op jit(solution)/shard_map/all_gather | solution.py:34
  62.9 0.0 collective-permute-done.5
  62.9 2.1 %all_gather.23.four_ref = bf16[64,3328]{1,0:T(8,128)(2,1)S(1)} all-gather(bf16[32,3328]{1,0:T(8,128)(2,1)S(1)} %collective-permute-done.5), channel_id=1, replica_groups={{0,16},{32,48},{64,80},{96,112},{128,144},{160,176},{192,208},{224,240}..., dimensions={0}, use_global_device_ids=true | all-gather | bytes 638976 | tf_op jit(solution)/shard_map/all_gather | solution.py:34
  65.0 0.0 collective-permute-done.4
  65.0 2.6 %all_gather.22.three_ref = bf16[128,3328]{1,0:T(8,128)(2,1)S(1)} all-gather(bf16[64,3328]{1,0:T(8,128)(2,1)} %collective-permute-done.4), channel_id=1, replica_groups={{0,16},{32,48},{64,80},{96,112},{128,144},{160,176},{192,208},{224,240}..., dimensions={0}, use_global_device_ids=true | all-gather | bytes 1277952 | tf_op jit(solution)/shard_map/all_gather | solution.py:34
  67.6 3.6 %all-to-all-done.1 = bf16[32,16,128]{2,1,0:T(8,128)(2,1)S(1)} async-done(((bf16[32,16,128]{2,1,0:T(8,128)(2,1)}), bf16[32,16,128]{2,1,0:T(8,128)(2,1)S(1)}, u32[]{:S(2)}, u32[]{:S(2)}) %all-to-all-start.1) | async-done | bytes 131104 | tf_op jit(solution)/shard_map/all_to_all | solution.py:172
  71.2 7.5 %export.1 = (bf16[512,3328]{1,0:T(8,128)(2,1)}, f32[4,26]{1,0:T(4,128)}, f32[64,3328]{1,0:T(8,128)}) custom-call(s32[2]{0:T(128)S(1)} %pad_add_fusion.at_ref, bf16[512,128]{1,0:T(8,128)(2,1)S(1)} %bitcast.6, bf16[64,3328]{1,0:T(8,128)(2,1)S(1)} %constant_dynamic-update-slice_fusion.own_ref, bf16[128,3328]{1,0:T(8,128)(2,1)S(1)} %all_gather.21.two_ref, ...), custom_call_target="tpu_custom_call" | custom-call | tf_op jit(solution)/shard_map/export/pallas_call | solution.py:119
  (3 shorter events, 0.0 us)
Async XLA Ops:
  2.3 14.3 %collective-permute-start = (bf16[16,3328]{1,0:T(8,128)(2,1)}, bf16[16,3328]{1,0:T(8,128)(2,1)S(1)}, u32[]{:S(2)}, u32[]{:S(2)}) collective-permute-start(bf16[16,3328]{1,0:T(8,128)(2,1)} %get-tuple-element.9), channel_id=1, source_target_pairs={{0,32},{16,48},{32,0},{48,16},{64,96},{80,112},{96,64},{112,80},{1... | collective-permute-start | bytes 319496 | tf_op jit(solution)/shard_map/ppermute | solution.py:156
  12.9 29.0 %collective-permute-start.2 = (bf16[32,3328]{1,0:T(8,128)(2,1)S(1)}, bf16[32,3328]{1,0:T(8,128)(2,1)S(1)}, u32[]{:S(2)}, u32[]{:S(2)}) collective-permute-start(bf16[32,3328]{1,0:T(8,128)(2,1)S(1)} %all_gather.19), channel_id=1, source_target_pairs={{0,128},{16,400},{32,160},{48,432},{64,192},{80,464},{96,224},{112... | collective-permute-start | bytes 638984 | tf_op jit(solution)/shard_map/ppermute | solution.py:158
  19.0 22.9 %collective-permute-start.3 = (bf16[32,3328]{1,0:T(8,128)(2,1)S(1)}, bf16[32,3328]{1,0:T(8,128)(2,1)S(1)}, u32[]{:S(2)}, u32[]{:S(2)}) collective-permute-start(bf16[32,3328]{1,0:T(8,128)(2,1)S(1)} %all_gather.18), channel_id=1, source_target_pairs={{0,128},{16,400},{32,160},{48,432},{64,192},{80,464},{96,224},{112... | collective-permute-start | bytes 638984 | tf_op jit(solution)/shard_map/ppermute | solution.py:160
  24.0 17.1 %all-to-all-start = ((bf16[16,16,4]{1,2,0:T(4,128)(2,1)}), bf16[16,16,4]{1,2,0:T(4,128)(2,1)S(1)}, u32[]{:S(2)}, u32[]{:S(2)}) async-start(bf16[16,16,4]{1,2,0:T(4,128)(2,1)} %broadcast_in_dim.4), calls=%async_computation | async-start | bytes 32768 | tf_op jit(solution)/shard_map/all_to_all | solution.py:164
  33.8 15.8 %collective-permute-start.1 = (bf16[64,3328]{1,0:T(8,128)(2,1)S(1)}, bf16[64,3328]{1,0:T(8,128)(2,1)S(1)}, u32[]{:S(2)}, u32[]{:S(2)}) collective-permute-start(bf16[64,3328]{1,0:T(8,128)(2,1)S(1)} %constant_dynamic-update-slice_fusion.own_ref), channel_id=1, source_target_pairs={{0,64},{16,464},{32,96},{48,496},{64,128},{80,16},{96,160},{112,48... | collective-permute-start | bytes 1277960 | tf_op jit(solution)/shard_map/ppermute | solution.py:162
  42.7 20.2 %collective-permute-start.5 = (bf16[32,3328]{1,0:T(8,128)(2,1)}, bf16[32,3328]{1,0:T(8,128)(2,1)S(1)}, u32[]{:S(2)}, u32[]{:S(2)}) collective-permute-start(bf16[32,3328]{1,0:T(8,128)(2,1)} %get-tuple-element.13), channel_id=1, source_target_pairs={{0,128},{16,400},{32,160},{48,432},{64,192},{80,464},{96,224},{112... | collective-permute-start | bytes 638984 | tf_op jit(solution)/shard_map/ppermute | solution.py:168
  45.4 19.6 %collective-permute-start.4 = (bf16[64,3328]{1,0:T(8,128)(2,1)S(1)}, bf16[64,3328]{1,0:T(8,128)(2,1)}, u32[]{:S(2)}, u32[]{:S(2)}) collective-permute-start(bf16[64,3328]{1,0:T(8,128)(2,1)S(1)} %get-tuple-element.12), channel_id=1, source_target_pairs={{0,64},{16,464},{32,96},{48,496},{64,128},{80,16},{96,160},{112,48... | collective-permute-start | bytes 1277960 | tf_op jit(solution)/shard_map/ppermute | solution.py:167
  53.1 18.2 %all-to-all-start.1 = ((bf16[32,16,128]{2,1,0:T(8,128)(2,1)}), bf16[32,16,128]{2,1,0:T(8,128)(2,1)S(1)}, u32[]{:S(2)}, u32[]{:S(2)}) async-start(bf16[32,16,128]{2,1,0:T(8,128)(2,1)} %broadcast_in_dim.5), calls=%async_computation.1 | async-start | bytes 262144 | tf_op jit(solution)/shard_map/all_to_all | solution.py:172

commit v2 on v0

v2 whole, which is shorter than its diff:
```python
import jax
import jax.numpy as jnp
from jax import lax
from jax.experimental import pallas as pl
from jax.experimental.pallas import tpu as pltpu
from jax.sharding import Mesh, PartitionSpec as P

BLOCK = 128
EPS = 1e-06
Y = 8
LANES = 128
HALF = 64
TILE = 256
MIB = 1024 * 1024


def along(a, step, across=0):
    pairs = []
    for y in range(Y):
        for xh in range(2):
            for core, to in ((0, (y + step) % Y), (1, (y - step) % Y)):
                pairs.append((y * 4 + xh * 2 + core, to * 4 + (xh ^ across) * 2 + core))
    return lax.ppermute(a, ("y", "x_hi", "core"), pairs)


def both_cores(a):
    return lax.all_gather(a, "core", axis=0, tiled=True)


def swap(a, axis):
    return lax.ppermute(a, axis, [(0, 1), (1, 0)])


def after(a, *others):
    return lax.optimization_barrier((a, *others))[0]


def kernel_of(body, out_shape, limit, cost=None, **more):
    params = pltpu.CompilerParams(vmem_limit_bytes=limit * MIB)
    if cost is not None:
        cost = pl.CostEstimate(flops=0, bytes_accessed=cost, transcendentals=0)
    return pl.pallas_call(body, out_shape=out_shape, compiler_params=params, cost_estimate=cost, name=body.__name__, **more)


def prepare(m_ref, x_ref):
    m = m_ref[...]
    rows, cols = m.shape
    x_ref[:, :cols] = m.astype(jnp.bfloat16)
    high = jnp.max(jnp.abs(m), axis=0, keepdims=True)
    lane = lax.broadcasted_iota(jnp.int32, (1, LANES), 1)
    tops = jnp.zeros((1, LANES), jnp.float32)
    for j in range(cols // BLOCK):
        top = jnp.max(high[:, j * BLOCK : (j + 1) * BLOCK], axis=1, keepdims=True)
        tops = jnp.where(lane == j, top, tops)
    first = tops.astype(jnp.bfloat16).astype(jnp.float32)
    second = (tops - first).astype(jnp.bfloat16).astype(jnp.float32)
    third = tops - first - second
    row = lax.broadcasted_iota(jnp.int32, (rows, LANES), 0)
    tail = jnp.where(row == 0, first, jnp.where(row == 1, second, third))
    x_ref[:, cols:] = jnp.where(row < 3, tail, 0.0).astype(jnp.bfloat16)


def spread(a_ref, out_ref):
    out_ref[...] = jnp.broadcast_to(a_ref[...][None], out_ref.shape)


def export(
    at_ref, a, b, two, one, three, four, codes_ref, scales_ref, probe_ref,
    codes_s, probe_s, tab_s, checks_s, scale_s, inv_s, sems, probe_sem,
):
    cols = codes_s.shape[1]
    n_blocks = cols // BLOCK
    y, xh = at_ref[0], at_ref[1]
    found = [(0, (a, 0), (b, 0))]
    for place, ref in ((2, two), (1, one), (3, three)):
        found += [(-place, (ref, 0), (ref, 32)), (place, (ref, 64), (ref, 96))]
    found.append((4, (four, 0), (four, 32)))

    def target(place, part):
        to = lax.rem(y + place + Y, Y)
        return to, pl.ds(pl.multiple_of(to * 64 + lax.rem(xh + part, 2) * 32, 32), 32)

    for place, *halves in found:
        for part, (ref, row) in enumerate(halves):
            tab_s[target(place, part)[1], :] = ref[row : row + 32, cols:].astype(jnp.float32)
    tab = tab_s[...]
    checks_s[...] = tab.T[HALF:, :].astype(jnp.bfloat16)
    terms = tab.reshape(32, 16, LANES)
    tops = terms[:, 0, :] + terms[:, 1, :] + terms[:, 2, :]
    scale = jnp.max(tops.reshape(4, 8, LANES), axis=1) + EPS
    scales_ref[...] = scale[:, :n_blocks]
    inv = 1.0 / scale
    for j in range(n_blocks):
        block = slice(j * BLOCK, (j + 1) * BLOCK)
        scale_s[:, block] = jnp.broadcast_to(scale[:, j : j + 1], (4, BLOCK))
        inv_s[:, block] = jnp.broadcast_to(inv[:, j : j + 1], (4, BLOCK))

    sends = []
    for n, (place, *halves) in enumerate(found):
        to = target(place, 0)[0]

        def strip(k, _, to=to, place=place, halves=halves):
            at = pl.ds(pl.multiple_of(k * TILE, TILE), TILE)
            factor = inv_s[pl.ds(to // 2, 1), at]
            for part, (ref, row) in enumerate(halves):
                value = ref[row : row + 32, at].astype(jnp.float32) * factor
                codes_s[target(place, part)[1], at] = value.astype(jnp.bfloat16)
            return 0

        lax.fori_loop(0, cols // TILE, strip, 0, unroll=True)
        rows = pl.ds(pl.multiple_of(to * 64, 64), 64)
        sends.append(pltpu.make_async_copy(codes_s.at[rows, :], codes_ref.at[rows, :], sems.at[n]))
        sends[-1].start()

    def dots(k, _):
        at = pl.ds(pl.multiple_of(k * TILE, TILE), TILE)
        total = jnp.zeros((HALF, TILE), jnp.float32)
        for g in range(4):
            group = slice(g * BLOCK, (g + 1) * BLOCK)
            part = jnp.dot(checks_s[:, group], codes_s[group, at], preferred_element_type=jnp.float32)
            total = total + part * scale_s[g : g + 1, at]
        probe_s[:, at] = total
        return 0

    lax.fori_loop(0, cols // TILE, dots, 0, unroll=True)
    sends.append(pltpu.make_async_copy(probe_s, probe_ref, probe_sem))
    sends[-1].start()
    for send in sends:
        send.wait()


SMEM = pl.BlockSpec(memory_space=pltpu.SMEM)
VMEM = pl.BlockSpec(memory_space=pltpu.VMEM)
ANY = pl.BlockSpec(memory_space=pl.ANY)


def per_device(master, checks):
    core, xh = lax.axis_index("core"), lax.axis_index("x_hi")
    at = jnp.stack([lax.axis_index("y"), xh, core]).astype(jnp.int32)
    rows, cols = master.shape
    n_blocks = cols // BLOCK
    full = lambda *shape: jax.ShapeDtypeStruct(shape, jnp.float32)
    brief = lambda *shape: jax.ShapeDtypeStruct(shape, jnp.bfloat16)

    peers = lax.axis_size("tensor")
    sent = kernel_of(spread, brief(peers, 4, rows), 4)(checks.T)
    got = lax.all_to_all(sent, "tensor", 0, 0).reshape(HALF, rows).T
    x = kernel_of(prepare, brief(rows, cols + LANES), 4)(master)
    a = both_cores(lax.dynamic_update_slice(x, got, (0, cols + HALF)))
    two_a, two_b = along(a, 2), along(a, 2, across=1)
    b = swap(a, "x_hi")
    one = along(jnp.concatenate([a, b], 0), 1)
    two = jnp.concatenate([two_a, two_b], 0)
    three = along(two, 1)
    four = along(jnp.where(core == 0, two_a, two_b), 2)

    two = both_cores(after(two, one))
    one = both_cores(one)
    four = both_cores(after(four, two, one))
    three = both_cores(after(three, four))
    return kernel_of(
        export,
        (brief(512, cols), full(4, n_blocks), full(HALF, cols)),
        16,
        in_specs=[SMEM] + [VMEM] * 6,
        out_specs=(ANY, VMEM, ANY),
        scratch_shapes=[
            pltpu.VMEM((512, cols), jnp.bfloat16),
            pltpu.VMEM((HALF, cols), jnp.float32),
            pltpu.VMEM((512, LANES), jnp.float32),
            pltpu.VMEM((HALF, 512), jnp.bfloat16),
            pltpu.VMEM((4, cols), jnp.float32),
            pltpu.VMEM((4, cols), jnp.float32),
            pltpu.SemaphoreType.DMA((8,)),
            pltpu.SemaphoreType.DMA,
        ],
    )(at, a, b, two, one, three, four)


def solution(mesh):
    split = Mesh(mesh.devices.reshape(Y, 2, 2, mesh.shape["tensor"]), ("y", "x_hi", "core", "tensor"))
    dp = ("y", "x_hi", "core")
    return jax.shard_map(
        per_device,
        mesh=split,
        in_specs=(P(dp, "tensor"), P(dp, "tensor")),
        out_specs=(P(None, "tensor"), P(None, "tensor"), P(None, "tensor")),
        check_vma=False,
    )
```

time: 178 us -> 70.3 us (0.39)
  blocking collectives: 83.8 us -> 15.5 us
  starting transfers between devices: 0.04 us -> 35.8 us
  local copies, waits for them, and re-layouts: 31.9 us -> 1.88 us
  waiting for transfers between devices: 28.1 us -> 11 us
  other arithmetic: 14.5 us -> 0.18 us
  between operations: 14.1 us -> 0.75 us
  matrix products: 5 us -> 0 us
  Pallas kernels: 0 us -> 4.77 us
    all_gather x2 -> x5, blocking collectives: 83.8 us -> 15.5 us  [both_cores(): return lax.all_gather(a, 'core', axis=0, tiled=True)]
    all_gather x1 -> x0, waiting for transfers between devices: 27.4 us -> none  [per_device(): lax.all_gather(master, 'dp', axis=0, tiled=True)]
    ppermute x0 -> x6, starting transfers between devices: none -> 23.9 us  [the longest x5 19.6 us: along(): return lax.ppermute(a, ('y', 'x_hi', 'core'), pairs)]
    abs x2 -> x0, local copies, waits for them, and re-layouts: 16.3 us -> none  [per_device(): scales = jnp.max(jnp.abs(tiles), axis=(1, 3)) + epsilon]
    all_to_all x0 -> x1, starting transfers between devices: none -> 11.9 us  [per_device(): got = lax.all_to_all(sent, 'tensor', 0, 0).reshape(HALF, rows).T]
    all_gather x1 -> x0, local copies, waits for them, and re-layouts: 7.64 us -> none  [per_device(): lax.all_gather(master, 'dp', axis=0, tiled=True)]
    all_to_all x0 -> x1, waiting for transfers between devices: none -> 6.28 us  [per_device(): got = lax.all_to_all(sent, 'tensor', 0, 0).reshape(HALF, rows).T]
    abs x1 -> x0, other arithmetic: 6.24 us -> none  [per_device(): scales = jnp.max(jnp.abs(tiles), axis=(1, 3)) + epsilon]
  transfers between devices with their start and end apart: 1 -> 7, of which waited for: 1 -> 3; matrix products, arithmetic and copies ran while one was open for 0% -> 0% of each run, Pallas kernels for 0% -> 0%
where the time goes in v2:
time: 70.3 us; the launch traced here: 69.9 us
  starting transfers between devices  35.8 us (51%)
  blocking collectives  15.5 us (22%)
  waiting for transfers between devices  11 us (16%)
  Pallas kernels  4.77 us (7%)
  local copies, waits for them, and re-layouts  1.88 us (3%)
  between operations  0.75 us (1%)
    ppermute x5, starting transfers between devices, along(): return lax.ppermute(a, ('y', 'x_hi', 'core'), pairs)  19.6 us
    all_gather x5, blocking collectives, both_cores(): return lax.all_gather(a, 'core', axis=0, tiled=True)  15.5 us
    all_to_all x1, starting transfers between devices, per_device(): got = lax.all_to_all(sent, 'tensor', 0, 0).reshape(HALF, rows).T  11.9 us
    all_to_all x1, waiting for transfers between devices, per_device(): got = lax.all_to_all(sent, 'tensor', 0, 0).reshape(HALF, rows).T  6.28 us
    ppermute x5, waiting for transfers between devices, along(): return lax.ppermute(a, ('y', 'x_hi', 'core'), pairs)  4.71 us
    ppermute x1, starting transfers between devices, swap(): return lax.ppermute(a, axis, [(0, 1), (1, 0)])  4.35 us
    pallas_call x1, Pallas kernels, per_device(): kernel_of(export, (brief(512, cols), full(4, n_blocks), full(HALF, cols))...  4.04 us
    unnamed x5, local copies, waits for them, and re-layouts  1.62 us
  transfers between devices with their start and end apart: 7, of which 3 were waited for; matrix products, arithmetic and copies ran while one was open for 0% of the time, Pallas kernels for 0%

profile of v2, /device:TPU:1, one launch (start us, length us, event | category | flops | bytes accessed | tf_op | source)
XLA Modules:
  0.0 69.9 jit_solution(11448946838801666544)
XLA Ops:
  0.6 0.0 copy-start.1
  0.6 0.7 copy-done.1
  1.3 0.6 spread.1
  1.9 11.9 %all-to-all-start = ((bf16[16,4,16]{2,1,0:T(4,128)(2,1)}), bf16[16,4,16]{2,1,0:T(4,128)(2,1)S(1)}, u32[]{:S(2)}, u32[]{:S(2)}) async-start(bf16[16,4,16]{2,1,0:T(4,128)(2,1)} %spread.1), calls=%async_computation | async-start | bytes 32768 | tf_op jit(solution)/shard_map/all_to_all | solution.py:147
  13.8 0.0 copy-start
  13.8 0.9 %copy-done = f32[16,3328]{1,0:T(8,128)S(1)} copy-done((f32[16,3328]{1,0:T(8,128)S(1)}, f32[16,3328]{1,0:T(8,128)}, u32[]{:S(2)}) %copy-start) | copy-done | bytes 213016
  14.8 0.1 prepare.1
  14.9 6.3 %all-to-all-done = bf16[16,4,16]{2,1,0:T(4,128)(2,1)S(1)} async-done(((bf16[16,4,16]{2,1,0:T(4,128)(2,1)}), bf16[16,4,16]{2,1,0:T(4,128)(2,1)S(1)}, u32[]{:S(2)}, u32[]{:S(2)}) %all-to-all-start) | async-done | bytes 2080 | tf_op jit(solution)/shard_map/all_to_all | solution.py:147
  21.2 0.1 copy.6
  21.2 0.2 dynamic_update_slice.3
  21.4 3.7 %all_gather.15.a = bf16[32,3456]{1,0:T(8,128)(2,1)S(1)} all-gather(bf16[16,3456]{1,0:T(8,128)(2,1)S(1)} %dynamic_update_slice.3), channel_id=1, replica_groups=mesh['y'=8,'x_hi'=2,'core'=2,'tensor'=16] {'core'}, dimensions={0}, use_global_device_ids=true | all-gather | bytes 331776 | tf_op jit(solution)/shard_map/all_gather | solution.py:27
  25.1 4.3 %collective-permute-start = (bf16[32,3456]{1,0:T(8,128)(2,1)S(1)}, bf16[32,3456]{1,0:T(8,128)(2,1)S(1)}, u32[]{:S(2)}, u32[]{:S(2)}) collective-permute-start(bf16[32,3456]{1,0:T(8,128)(2,1)S(1)} %all_gather.15.a), channel_id=1, source_target_pairs={{0,32},{32,0},{1,33},{33,1},{2,34},{34,2},{3,35},{35,3},{4,36},{36... | collective-permute-start | bytes 663560 | tf_op jit(solution)/shard_map/ppermute | solution.py:31
  29.5 0.1 pad_add_fusion.at_ref
  29.6 6.1 %collective-permute-start.2 = (bf16[32,3456]{1,0:T(8,128)(2,1)S(1)}, bf16[32,3456]{1,0:T(8,128)(2,1)S(1)}, u32[]{:S(2)}, u32[]{:S(2)}) collective-permute-start(bf16[32,3456]{1,0:T(8,128)(2,1)S(1)} %all_gather.15.a), channel_id=1, source_target_pairs={{0,160},{16,432},{32,128},{48,400},{64,224},{80,496},{96,192},{112... | collective-permute-start | bytes 663560 | tf_op jit(solution)/shard_map/ppermute | solution.py:23
  35.7 3.8 %collective-permute-start.1 = (bf16[32,3456]{1,0:T(8,128)(2,1)S(1)}, bf16[32,3456]{1,0:T(8,128)(2,1)S(1)}, u32[]{:S(2)}, u32[]{:S(2)}) collective-permute-start(bf16[32,3456]{1,0:T(8,128)(2,1)S(1)} %all_gather.15.a), channel_id=1, source_target_pairs={{0,128},{16,400},{32,160},{48,432},{64,192},{80,464},{96,224},{112... | collective-permute-start | bytes 663560 | tf_op jit(solution)/shard_map/ppermute | solution.py:23
  39.5 0.0 collective-permute-done.b
  39.5 2.1 %collective-permute-start.3 = (bf16[64,3456]{1,0:T(8,128)(2,1)S(1)}, bf16[64,3456]{1,0:T(8,128)(2,1)S(1)}, u32[]{:S(2)}, u32[]{:S(2)}) collective-permute-start(bf16[64,3456]{1,0:T(8,128)(2,1)S(1)} %pad_maximum_fusion), channel_id=1, source_target_pairs={{0,64},{16,464},{32,96},{48,496},{64,128},{80,16},{96,160},{112,48... | collective-permute-start | bytes 1327112 | tf_op jit(solution)/shard_map/ppermute | solution.py:23
  41.6 4.3 %collective-permute-done.1 = bf16[32,3456]{1,0:T(8,128)(2,1)S(1)} collective-permute-done((bf16[32,3456]{1,0:T(8,128)(2,1)S(1)}, bf16[32,3456]{1,0:T(8,128)(2,1)S(1)}, u32[]{:S(2)}, u32[]{:S(2)}) %collective-permute-start.1) | collective-permute-done | bytes 221216 | tf_op jit(solution)/shard_map/ppermute | solution.py:23
  46.0 0.0 collective-permute-done.2
  46.0 0.1 broadcast_select_fusion
  46.0 5.7 %collective-permute-start.5 = (bf16[32,3456]{1,0:T(8,128)(2,1)S(1)}, bf16[32,3456]{1,0:T(8,128)(2,1)S(1)}, u32[]{:S(2)}, u32[]{:S(2)}) collective-permute-start(bf16[32,3456]{1,0:T(8,128)(2,1)S(1)} %get-tuple-element.9), channel_id=1, source_target_pairs={{0,128},{16,400},{32,160},{48,432},{64,192},{80,464},{96,224},{112... | collective-permute-start | bytes 663560 | tf_op jit(solution)/shard_map/ppermute | solution.py:23
  51.7 1.9 %collective-permute-start.4 = (bf16[64,3456]{1,0:T(8,128)(2,1)S(1)}, bf16[64,3456]{1,0:T(8,128)(2,1)S(1)}, u32[]{:S(2)}, u32[]{:S(2)}) collective-permute-start(bf16[64,3456]{1,0:T(8,128)(2,1)S(1)} %get-tuple-element.6), channel_id=1, source_target_pairs={{0,64},{16,464},{32,96},{48,496},{64,128},{80,16},{96,160},{112,48... | collective-permute-start | bytes 1327112 | tf_op jit(solution)/shard_map/ppermute | solution.py:23
  53.7 0.0 collective-permute-done.3
  53.7 2.4 %all_gather.16.two = bf16[128,3456]{1,0:T(8,128)(2,1)S(1)} all-gather(bf16[64,3456]{1,0:T(8,128)(2,1)S(1)} %get-tuple-element.6), channel_id=1, replica_groups=mesh['y'=8,'x_hi'=2,'core'=2,'tensor'=16] {'core'}, dimensions={0}, use_global_device_ids=true | all-gather | bytes 1327104 | tf_op jit(solution)/shard_map/all_gather | solution.py:27
  56.1 2.4 %all_gather.17.one = bf16[128,3456]{1,0:T(8,128)(2,1)S(1)} all-gather(bf16[64,3456]{1,0:T(8,128)(2,1)S(1)} %collective-permute-done.3), channel_id=1, replica_groups=mesh['y'=8,'x_hi'=2,'core'=2,'tensor'=16] {'core'}, dimensions={0}, use_global_device_ids=true | all-gather | bytes 1327104 | tf_op jit(solution)/shard_map/all_gather | solution.py:27
  58.6 0.0 collective-permute-done.5
  58.6 2.2 %all_gather.18.four = bf16[64,3456]{1,0:T(8,128)(2,1)S(1)} all-gather(bf16[32,3456]{1,0:T(8,128)(2,1)S(1)} %collective-permute-done.5), channel_id=1, replica_groups=mesh['y'=8,'x_hi'=2,'core'=2,'tensor'=16] {'core'}, dimensions={0}, use_global_device_ids=true | all-gather | bytes 663552 | tf_op jit(solution)/shard_map/all_gather | solution.py:27
  60.7 0.4 collective-permute-done.4
  61.1 4.8 %all_gather.19.three = bf16[128,3456]{1,0:T(8,128)(2,1)S(1)} all-gather(bf16[64,3456]{1,0:T(8,128)(2,1)S(1)} %collective-permute-done.4), channel_id=1, replica_groups=mesh['y'=8,'x_hi'=2,'core'=2,'tensor'=16] {'core'}, dimensions={0}, use_global_device_ids=true | all-gather | bytes 1327104 | tf_op jit(solution)/shard_map/all_gather | solution.py:27
  65.9 4.0 %export.1 = (bf16[512,3328]{1,0:T(8,128)(2,1)}, f32[4,26]{1,0:T(4,128)}, f32[64,3328]{1,0:T(8,128)}) custom-call(s32[3]{0:T(128)S(1)} %pad_add_fusion.at_ref, bf16[32,3456]{1,0:T(8,128)(2,1)S(1)} %all_gather.15.a, bf16[32,3456]{1,0:T(8,128)(2,1)S(1)} %collective-permute-done.b, bf16[128,3456]{1,0:T(8,128)(2,1)S(1)} %all_gather.16.two, ...), custom_call_target="tpu_custom_call" | custom-call | tf_op jit(solution)/shard_map/export/pallas_call | solution.py:161
  (2 shorter events, 0.1 us)
Async XLA Ops:
  0.6 0.7 copy-start.1
  1.9 19.2 %all-to-all-start = ((bf16[16,4,16]{2,1,0:T(4,128)(2,1)}), bf16[16,4,16]{2,1,0:T(4,128)(2,1)S(1)}, u32[]{:S(2)}, u32[]{:S(2)}) async-start(bf16[16,4,16]{2,1,0:T(4,128)(2,1)} %spread.1), calls=%async_computation | async-start | bytes 32768 | tf_op jit(solution)/shard_map/all_to_all | solution.py:147
  13.8 0.9 %copy-start = (f32[16,3328]{1,0:T(8,128)S(1)}, f32[16,3328]{1,0:T(8,128)}, u32[]{:S(2)}) copy-start(f32[16,3328]{1,0:T(8,128)} %m_ref.1) | copy-start | bytes 638980
  25.1 14.3 %collective-permute-start = (bf16[32,3456]{1,0:T(8,128)(2,1)S(1)}, bf16[32,3456]{1,0:T(8,128)(2,1)S(1)}, u32[]{:S(2)}, u32[]{:S(2)}) collective-permute-start(bf16[32,3456]{1,0:T(8,128)(2,1)S(1)} %all_gather.15.a), channel_id=1, source_target_pairs={{0,32},{32,0},{1,33},{33,1},{2,34},{34,2},{3,35},{35,3},{4,36},{36... | collective-permute-start | bytes 663560 | tf_op jit(solution)/shard_map/ppermute | solution.py:31
  29.6 16.4 %collective-permute-start.2 = (bf16[32,3456]{1,0:T(8,128)(2,1)S(1)}, bf16[32,3456]{1,0:T(8,128)(2,1)S(1)}, u32[]{:S(2)}, u32[]{:S(2)}) collective-permute-start(bf16[32,3456]{1,0:T(8,128)(2,1)S(1)} %all_gather.15.a), channel_id=1, source_target_pairs={{0,160},{16,432},{32,128},{48,400},{64,224},{80,496},{96,192},{112... | collective-permute-start | bytes 663560 | tf_op jit(solution)/shard_map/ppermute | solution.py:23
  35.7 10.2 %collective-permute-start.1 = (bf16[32,3456]{1,0:T(8,128)(2,1)S(1)}, bf16[32,3456]{1,0:T(8,128)(2,1)S(1)}, u32[]{:S(2)}, u32[]{:S(2)}) collective-permute-start(bf16[32,3456]{1,0:T(8,128)(2,1)S(1)} %all_gather.15.a), channel_id=1, source_target_pairs={{0,128},{16,400},{32,160},{48,432},{64,192},{80,464},{96,224},{112... | collective-permute-start | bytes 663560 | tf_op jit(solution)/shard_map/ppermute | solution.py:23
  39.5 14.2 %collective-permute-start.3 = (bf16[64,3456]{1,0:T(8,128)(2,1)S(1)}, bf16[64,3456]{1,0:T(8,128)(2,1)S(1)}, u32[]{:S(2)}, u32[]{:S(2)}) collective-permute-start(bf16[64,3456]{1,0:T(8,128)(2,1)S(1)} %pad_maximum_fusion), channel_id=1, source_target_pairs={{0,64},{16,464},{32,96},{48,496},{64,128},{80,16},{96,160},{112,48... | collective-permute-start | bytes 1327112 | tf_op jit(solution)/shard_map/ppermute | solution.py:23
  46.0 12.5 %collective-permute-start.5 = (bf16[32,3456]{1,0:T(8,128)(2,1)S(1)}, bf16[32,3456]{1,0:T(8,128)(2,1)S(1)}, u32[]{:S(2)}, u32[]{:S(2)}) collective-permute-start(bf16[32,3456]{1,0:T(8,128)(2,1)S(1)} %get-tuple-element.9), channel_id=1, source_target_pairs={{0,128},{16,400},{32,160},{48,432},{64,192},{80,464},{96,224},{112... | collective-permute-start | bytes 663560 | tf_op jit(solution)/shard_map/ppermute | solution.py:23
  51.7 9.3 %collective-permute-start.4 = (bf16[64,3456]{1,0:T(8,128)(2,1)S(1)}, bf16[64,3456]{1,0:T(8,128)(2,1)S(1)}, u32[]{:S(2)}, u32[]{:S(2)}) collective-permute-start(bf16[64,3456]{1,0:T(8,128)(2,1)S(1)} %get-tuple-element.6), channel_id=1, source_target_pairs={{0,64},{16,464},{32,96},{48,496},{64,128},{80,16},{96,160},{112,48... | collective-permute-start | bytes 1327112 | tf_op jit(solution)/shard_map/ppermute | solution.py:23

commit v3 on v2

--- a/solution.py
+++ b/solution.py
@@ -12,6 +12,7 @@
 HALF = 64
 TILE = 256
 MIB = 1024 * 1024
+TOP = 255.0 * 2.0**120
 
 
 def along(a, step, across=0):
@@ -45,14 +46,14 @@
 def prepare(m_ref, x_ref):
     m = m_ref[...]
     rows, cols = m.shape
-    x_ref[:, :cols] = m.astype(jnp.bfloat16)
+    x_ref[:, :cols] = jnp.clip(m, -TOP, TOP).astype(jnp.bfloat16)
     high = jnp.max(jnp.abs(m), axis=0, keepdims=True)
     lane = lax.broadcasted_iota(jnp.int32, (1, LANES), 1)
     tops = jnp.zeros((1, LANES), jnp.float32)
     for j in range(cols // BLOCK):
         top = jnp.max(high[:, j * BLOCK : (j + 1) * BLOCK], axis=1, keepdims=True)
         tops = jnp.where(lane == j, top, tops)
-    first = tops.astype(jnp.bfloat16).astype(jnp.float32)
+    first = jnp.minimum(tops, TOP).astype(jnp.bfloat16).astype(jnp.float32)
     second = (tops - first).astype(jnp.bfloat16).astype(jnp.float32)
     third = tops - first - second
     row = lax.broadcasted_iota(jnp.int32, (rows, LANES), 0)
@@ -71,6 +72,7 @@
     cols = codes_s.shape[1]
     n_blocks = cols // BLOCK
     y, xh = at_ref[0], at_ref[1]
+    shrink = lambda scale: jnp.where(scale > 2.0**100, 2.0**-60, 1.0)
     found = [(0, (a, 0), (b, 0))]
     for place, ref in ((2, two), (1, one), (3, three)):
         found += [(-place, (ref, 0), (ref, 32)), (place, (ref, 64), (ref, 96))]
@@ -86,33 +88,43 @@
     tab = tab_s[...]
     checks_s[...] = tab.T[HALF:, :].astype(jnp.bfloat16)
     terms = tab.reshape(32, 16, LANES)
-    tops = terms[:, 0, :] + terms[:, 1, :] + terms[:, 2, :]
+    tops = terms[:, 0, :] + (terms[:, 1, :] + terms[:, 2, :])
     scale = jnp.max(tops.reshape(4, 8, LANES), axis=1) + EPS
     scales_ref[...] = scale[:, :n_blocks]
-    inv = 1.0 / scale
     for j in range(n_blocks):
         block = slice(j * BLOCK, (j + 1) * BLOCK)
-        scale_s[:, block] = jnp.broadcast_to(scale[:, j : j + 1], (4, BLOCK))
-        inv_s[:, block] = jnp.broadcast_to(inv[:, j : j + 1], (4, BLOCK))
-
+        wide = jnp.broadcast_to(scale[:, j : j + 1], (4, BLOCK))
+        scale_s[:, block] = wide
+        inv_s[:, block] = 1.0 / (wide * shrink(wide))
+
+    large = jnp.max(scale) > 2.0**100
     sends = []
     for n, (place, *halves) in enumerate(found):
         to = target(place, 0)[0]
-
-        def strip(k, _, to=to, place=place, halves=halves):
+        group = to // 2
+        dests = [target(place, part)[1] for part in (0, 1)]
+
+        def strip(k, shrunk, group=group, dests=dests, halves=halves):
             at = pl.ds(pl.multiple_of(k * TILE, TILE), TILE)
-            factor = inv_s[pl.ds(to // 2, 1), at]
-            for part, (ref, row) in enumerate(halves):
-                value = ref[row : row + 32, at].astype(jnp.float32) * factor
-                codes_s[target(place, part)[1], at] = value.astype(jnp.bfloat16)
-            return 0
-
-        lax.fori_loop(0, cols // TILE, strip, 0, unroll=True)
+            factor = inv_s[pl.ds(group, 1), at]
+            for dest, (ref, row) in zip(dests, halves):
+                value = ref[row : row + 32, at].astype(jnp.float32)
+                if shrunk:
+                    value = value * shrink(scale_s[pl.ds(group, 1), at])
+                codes_s[dest, at] = (value * factor).astype(jnp.bfloat16)
+
+        for k in range(cols // TILE):
+            strip(k, False)
+
+        @pl.when(large)
+        def _(strip=strip):
+            pl.loop(0, cols // TILE)(lambda k: strip(k, True))
+
         rows = pl.ds(pl.multiple_of(to * 64, 64), 64)
         sends.append(pltpu.make_async_copy(codes_s.at[rows, :], codes_ref.at[rows, :], sems.at[n]))
         sends[-1].start()
 
-    def dots(k, _):
+    def dots(k):
         at = pl.ds(pl.multiple_of(k * TILE, TILE), TILE)
         total = jnp.zeros((HALF, TILE), jnp.float32)
         for g in range(4):
@@ -120,11 +132,15 @@
             part = jnp.dot(checks_s[:, group], codes_s[group, at], preferred_element_type=jnp.float32)
             total = total + part * scale_s[g : g + 1, at]
         probe_s[:, at] = total
-        return 0
-
-    lax.fori_loop(0, cols // TILE, dots, 0, unroll=True)
-    sends.append(pltpu.make_async_copy(probe_s, probe_ref, probe_sem))
-    sends[-1].start()
+
+    strips, done = cols // TILE, 0
+    for n, upto in enumerate((strips // 2, strips)):
+        for k in range(done, upto):
+            dots(k)
+        at = slice(done * TILE, upto * TILE)
+        sends.append(pltpu.make_async_copy(probe_s.at[:, at], probe_ref.at[:, at], probe_sem.at[n]))
+        sends[-1].start()
+        done = upto
     for send in sends:
         send.wait()
 
@@ -172,7 +188,7 @@
             pltpu.VMEM((4, cols), jnp.float32),
             pltpu.VMEM((4, cols), jnp.float32),
             pltpu.SemaphoreType.DMA((8,)),
-            pltpu.SemaphoreType.DMA,
+            pltpu.SemaphoreType.DMA((2,)),
         ],
     )(at, a, b, two, one, three, four)
 

time: 70.3 us -> 70 us (level)
  no operation moved by 1% of the time
where the time goes in v3:
time: 70 us; the launch traced here: 69.6 us
  starting transfers between devices  35.8 us (51%)
  blocking collectives  15.5 us (22%)
  waiting for transfers between devices  11 us (16%)
  Pallas kernels  4.43 us (6%)
  local copies, waits for them, and re-layouts  1.88 us (3%)
  between operations  0.75 us (1%)
    ppermute x5, starting transfers between devices, along(): return lax.ppermute(a, ('y', 'x_hi', 'core'), pairs)  19.6 us
    all_gather x5, blocking collectives, both_cores(): return lax.all_gather(a, 'core', axis=0, tiled=True)  15.5 us
    all_to_all x1, starting transfers between devices, per_device(): got = lax.all_to_all(sent, 'tensor', 0, 0).reshape(HALF, rows).T  11.9 us
    all_to_all x1, waiting for transfers between devices, per_device(): got = lax.all_to_all(sent, 'tensor', 0, 0).reshape(HALF, rows).T  6.27 us
    ppermute x5, waiting for transfers between devices, along(): return lax.ppermute(a, ('y', 'x_hi', 'core'), pairs)  4.71 us
    ppermute x1, starting transfers between devices, swap(): return lax.ppermute(a, axis, [(0, 1), (1, 0)])  4.35 us
    pallas_call x1, Pallas kernels, per_device(): kernel_of(export, (brief(512, cols), full(4, n_blocks), full(HALF, cols))...  3.7 us
    unnamed x5, local copies, waits for them, and re-layouts  1.62 us
  transfers between devices with their start and end apart: 7, of which 3 were waited for; matrix products, arithmetic and copies ran while one was open for 0% of the time, Pallas kernels for 0%

profile of v3, /device:TPU:1, one launch (start us, length us, event | category | flops | bytes accessed | tf_op | source)
XLA Modules:
  0.0 69.6 jit_solution(18113974978779979636)
XLA Ops:
  0.6 0.0 copy-start.1
  0.6 0.7 copy-done.1
  1.3 0.6 spread.1
  1.9 11.9 %all-to-all-start = ((bf16[16,4,16]{2,1,0:T(4,128)(2,1)}), bf16[16,4,16]{2,1,0:T(4,128)(2,1)S(1)}, u32[]{:S(2)}, u32[]{:S(2)}) async-start(bf16[16,4,16]{2,1,0:T(4,128)(2,1)} %spread.1), calls=%async_computation | async-start | bytes 32768 | tf_op jit(solution)/shard_map/all_to_all | solution.py:163
  13.8 0.0 copy-start
  13.8 0.9 %copy-done = f32[16,3328]{1,0:T(8,128)S(1)} copy-done((f32[16,3328]{1,0:T(8,128)S(1)}, f32[16,3328]{1,0:T(8,128)}, u32[]{:S(2)}) %copy-start) | copy-done | bytes 213016
  14.8 0.1 prepare.1
  14.9 6.3 %all-to-all-done = bf16[16,4,16]{2,1,0:T(4,128)(2,1)S(1)} async-done(((bf16[16,4,16]{2,1,0:T(4,128)(2,1)}), bf16[16,4,16]{2,1,0:T(4,128)(2,1)S(1)}, u32[]{:S(2)}, u32[]{:S(2)}) %all-to-all-start) | async-done | bytes 2080 | tf_op jit(solution)/shard_map/all_to_all | solution.py:163
  21.2 0.1 copy.6
  21.2 0.2 dynamic_update_slice.3
  21.4 3.7 %all_gather.15.a = bf16[32,3456]{1,0:T(8,128)(2,1)S(1)} all-gather(bf16[16,3456]{1,0:T(8,128)(2,1)S(1)} %dynamic_update_slice.3), channel_id=1, replica_groups=mesh['y'=8,'x_hi'=2,'core'=2,'tensor'=16] {'core'}, dimensions={0}, use_global_device_ids=true | all-gather | bytes 331776 | tf_op jit(solution)/shard_map/all_gather | solution.py:28
  25.1 4.3 %collective-permute-start = (bf16[32,3456]{1,0:T(8,128)(2,1)S(1)}, bf16[32,3456]{1,0:T(8,128)(2,1)S(1)}, u32[]{:S(2)}, u32[]{:S(2)}) collective-permute-start(bf16[32,3456]{1,0:T(8,128)(2,1)S(1)} %all_gather.15.a), channel_id=1, source_target_pairs={{0,32},{32,0},{1,33},{33,1},{2,34},{34,2},{3,35},{35,3},{4,36},{36... | collective-permute-start | bytes 663560 | tf_op jit(solution)/shard_map/ppermute | solution.py:32
  29.5 0.1 pad_add_fusion.at_ref
  29.6 6.1 %collective-permute-start.2 = (bf16[32,3456]{1,0:T(8,128)(2,1)S(1)}, bf16[32,3456]{1,0:T(8,128)(2,1)S(1)}, u32[]{:S(2)}, u32[]{:S(2)}) collective-permute-start(bf16[32,3456]{1,0:T(8,128)(2,1)S(1)} %all_gather.15.a), channel_id=1, source_target_pairs={{0,160},{16,432},{32,128},{48,400},{64,224},{80,496},{96,192},{112... | collective-permute-start | bytes 663560 | tf_op jit(solution)/shard_map/ppermute | solution.py:24
  35.7 3.8 %collective-permute-start.1 = (bf16[32,3456]{1,0:T(8,128)(2,1)S(1)}, bf16[32,3456]{1,0:T(8,128)(2,1)S(1)}, u32[]{:S(2)}, u32[]{:S(2)}) collective-permute-start(bf16[32,3456]{1,0:T(8,128)(2,1)S(1)} %all_gather.15.a), channel_id=1, source_target_pairs={{0,128},{16,400},{32,160},{48,432},{64,192},{80,464},{96,224},{112... | collective-permute-start | bytes 663560 | tf_op jit(solution)/shard_map/ppermute | solution.py:24
  39.5 0.0 collective-permute-done.b
  39.5 2.1 %collective-permute-start.3 = (bf16[64,3456]{1,0:T(8,128)(2,1)S(1)}, bf16[64,3456]{1,0:T(8,128)(2,1)S(1)}, u32[]{:S(2)}, u32[]{:S(2)}) collective-permute-start(bf16[64,3456]{1,0:T(8,128)(2,1)S(1)} %pad_maximum_fusion), channel_id=1, source_target_pairs={{0,64},{16,464},{32,96},{48,496},{64,128},{80,16},{96,160},{112,48... | collective-permute-start | bytes 1327112 | tf_op jit(solution)/shard_map/ppermute | solution.py:24
  41.6 4.3 %collective-permute-done.1 = bf16[32,3456]{1,0:T(8,128)(2,1)S(1)} collective-permute-done((bf16[32,3456]{1,0:T(8,128)(2,1)S(1)}, bf16[32,3456]{1,0:T(8,128)(2,1)S(1)}, u32[]{:S(2)}, u32[]{:S(2)}) %collective-permute-start.1) | collective-permute-done | bytes 221216 | tf_op jit(solution)/shard_map/ppermute | solution.py:24
  46.0 0.0 collective-permute-done.2
  46.0 0.1 broadcast_select_fusion
  46.0 5.7 %collective-permute-start.5 = (bf16[32,3456]{1,0:T(8,128)(2,1)S(1)}, bf16[32,3456]{1,0:T(8,128)(2,1)S(1)}, u32[]{:S(2)}, u32[]{:S(2)}) collective-permute-start(bf16[32,3456]{1,0:T(8,128)(2,1)S(1)} %get-tuple-element.9), channel_id=1, source_target_pairs={{0,128},{16,400},{32,160},{48,432},{64,192},{80,464},{96,224},{112... | collective-permute-start | bytes 663560 | tf_op jit(solution)/shard_map/ppermute | solution.py:24
  51.7 1.9 %collective-permute-start.4 = (bf16[64,3456]{1,0:T(8,128)(2,1)S(1)}, bf16[64,3456]{1,0:T(8,128)(2,1)S(1)}, u32[]{:S(2)}, u32[]{:S(2)}) collective-permute-start(bf16[64,3456]{1,0:T(8,128)(2,1)S(1)} %get-tuple-element.6), channel_id=1, source_target_pairs={{0,64},{16,464},{32,96},{48,496},{64,128},{80,16},{96,160},{112,48... | collective-permute-start | bytes 1327112 | tf_op jit(solution)/shard_map/ppermute | solution.py:24
  53.7 0.0 collective-permute-done.3
  53.7 2.4 %all_gather.16.two = bf16[128,3456]{1,0:T(8,128)(2,1)S(1)} all-gather(bf16[64,3456]{1,0:T(8,128)(2,1)S(1)} %get-tuple-element.6), channel_id=1, replica_groups=mesh['y'=8,'x_hi'=2,'core'=2,'tensor'=16] {'core'}, dimensions={0}, use_global_device_ids=true | all-gather | bytes 1327104 | tf_op jit(solution)/shard_map/all_gather | solution.py:28
  56.1 2.4 %all_gather.17.one = bf16[128,3456]{1,0:T(8,128)(2,1)S(1)} all-gather(bf16[64,3456]{1,0:T(8,128)(2,1)S(1)} %collective-permute-done.3), channel_id=1, replica_groups=mesh['y'=8,'x_hi'=2,'core'=2,'tensor'=16] {'core'}, dimensions={0}, use_global_device_ids=true | all-gather | bytes 1327104 | tf_op jit(solution)/shard_map/all_gather | solution.py:28
  58.6 0.0 collective-permute-done.5
  58.6 2.2 %all_gather.18.four = bf16[64,3456]{1,0:T(8,128)(2,1)S(1)} all-gather(bf16[32,3456]{1,0:T(8,128)(2,1)S(1)} %collective-permute-done.5), channel_id=1, replica_groups=mesh['y'=8,'x_hi'=2,'core'=2,'tensor'=16] {'core'}, dimensions={0}, use_global_device_ids=true | all-gather | bytes 663552 | tf_op jit(solution)/shard_map/all_gather | solution.py:28
  60.7 0.4 collective-permute-done.4
  61.1 4.8 %all_gather.19.three = bf16[128,3456]{1,0:T(8,128)(2,1)S(1)} all-gather(bf16[64,3456]{1,0:T(8,128)(2,1)S(1)} %collective-permute-done.4), channel_id=1, replica_groups=mesh['y'=8,'x_hi'=2,'core'=2,'tensor'=16] {'core'}, dimensions={0}, use_global_device_ids=true | all-gather | bytes 1327104 | tf_op jit(solution)/shard_map/all_gather | solution.py:28
  65.9 3.7 %export.1 = (bf16[512,3328]{1,0:T(8,128)(2,1)}, f32[4,26]{1,0:T(4,128)}, f32[64,3328]{1,0:T(8,128)}) custom-call(s32[3]{0:T(128)S(1)} %pad_add_fusion.at_ref, bf16[32,3456]{1,0:T(8,128)(2,1)S(1)} %all_gather.15.a, bf16[32,3456]{1,0:T(8,128)(2,1)S(1)} %collective-permute-done.b, bf16[128,3456]{1,0:T(8,128)(2,1)S(1)} %all_gather.16.two, ...), custom_call_target="tpu_custom_call" | custom-call | tf_op jit(solution)/shard_map/export/pallas_call | solution.py:177
  (2 shorter events, 0.1 us)
Async XLA Ops:
  0.6 0.7 copy-start.1
  1.9 19.2 %all-to-all-start = ((bf16[16,4,16]{2,1,0:T(4,128)(2,1)}), bf16[16,4,16]{2,1,0:T(4,128)(2,1)S(1)}, u32[]{:S(2)}, u32[]{:S(2)}) async-start(bf16[16,4,16]{2,1,0:T(4,128)(2,1)} %spread.1), calls=%async_computation | async-start | bytes 32768 | tf_op jit(solution)/shard_map/all_to_all | solution.py:163
  13.8 0.9 %copy-start = (f32[16,3328]{1,0:T(8,128)S(1)}, f32[16,3328]{1,0:T(8,128)}, u32[]{:S(2)}) copy-start(f32[16,3328]{1,0:T(8,128)} %m_ref.1) | copy-start | bytes 638980
  25.1 14.3 %collective-permute-start = (bf16[32,3456]{1,0:T(8,128)(2,1)S(1)}, bf16[32,3456]{1,0:T(8,128)(2,1)S(1)}, u32[]{:S(2)}, u32[]{:S(2)}) collective-permute-start(bf16[32,3456]{1,0:T(8,128)(2,1)S(1)} %all_gather.15.a), channel_id=1, source_target_pairs={{0,32},{32,0},{1,33},{33,1},{2,34},{34,2},{3,35},{35,3},{4,36},{36... | collective-permute-start | bytes 663560 | tf_op jit(solution)/shard_map/ppermute | solution.py:32
  29.6 16.4 %collective-permute-start.2 = (bf16[32,3456]{1,0:T(8,128)(2,1)S(1)}, bf16[32,3456]{1,0:T(8,128)(2,1)S(1)}, u32[]{:S(2)}, u32[]{:S(2)}) collective-permute-start(bf16[32,3456]{1,0:T(8,128)(2,1)S(1)} %all_gather.15.a), channel_id=1, source_target_pairs={{0,160},{16,432},{32,128},{48,400},{64,224},{80,496},{96,192},{112... | collective-permute-start | bytes 663560 | tf_op jit(solution)/shard_map/ppermute | solution.py:24
  35.7 10.2 %collective-permute-start.1 = (bf16[32,3456]{1,0:T(8,128)(2,1)S(1)}, bf16[32,3456]{1,0:T(8,128)(2,1)S(1)}, u32[]{:S(2)}, u32[]{:S(2)}) collective-permute-start(bf16[32,3456]{1,0:T(8,128)(2,1)S(1)} %all_gather.15.a), channel_id=1, source_target_pairs={{0,128},{16,400},{32,160},{48,432},{64,192},{80,464},{96,224},{112... | collective-permute-start | bytes 663560 | tf_op jit(solution)/shard_map/ppermute | solution.py:24
  39.5 14.2 %collective-permute-start.3 = (bf16[64,3456]{1,0:T(8,128)(2,1)S(1)}, bf16[64,3456]{1,0:T(8,128)(2,1)S(1)}, u32[]{:S(2)}, u32[]{:S(2)}) collective-permute-start(bf16[64,3456]{1,0:T(8,128)(2,1)S(1)} %pad_maximum_fusion), channel_id=1, source_target_pairs={{0,64},{16,464},{32,96},{48,496},{64,128},{80,16},{96,160},{112,48... | collective-permute-start | bytes 1327112 | tf_op jit(solution)/shard_map/ppermute | solution.py:24
  46.0 12.5 %collective-permute-start.5 = (bf16[32,3456]{1,0:T(8,128)(2,1)S(1)}, bf16[32,3456]{1,0:T(8,128)(2,1)S(1)}, u32[]{:S(2)}, u32[]{:S(2)}) collective-permute-start(bf16[32,3456]{1,0:T(8,128)(2,1)S(1)} %get-tuple-element.9), channel_id=1, source_target_pairs={{0,128},{16,400},{32,160},{48,432},{64,192},{80,464},{96,224},{112... | collective-permute-start | bytes 663560 | tf_op jit(solution)/shard_map/ppermute | solution.py:24
  51.7 9.3 %collective-permute-start.4 = (bf16[64,3456]{1,0:T(8,128)(2,1)S(1)}, bf16[64,3456]{1,0:T(8,128)(2,1)S(1)}, u32[]{:S(2)}, u32[]{:S(2)}) collective-permute-start(bf16[64,3456]{1,0:T(8,128)(2,1)S(1)} %get-tuple-element.6), channel_id=1, source_target_pairs={{0,64},{16,464},{32,96},{48,496},{64,128},{80,16},{96,160},{112,48... | collective-permute-start | bytes 1327112 | tf_op jit(solution)/shard_map/ppermute | solution.py:24

commit v4 on v3

--- a/solution.py
+++ b/solution.py
@@ -19,7 +19,7 @@
     pairs = []
     for y in range(Y):
         for xh in range(2):
-            for core, to in ((0, (y + step) % Y), (1, (y - step) % Y)):
+            for core, to in ((0, (y - step) % Y), (1, (y + step) % Y)):
                 pairs.append((y * 4 + xh * 2 + core, to * 4 + (xh ^ across) * 2 + core))
     return lax.ppermute(a, ("y", "x_hi", "core"), pairs)
 
@@ -75,7 +75,7 @@
     shrink = lambda scale: jnp.where(scale > 2.0**100, 2.0**-60, 1.0)
     found = [(0, (a, 0), (b, 0))]
     for place, ref in ((2, two), (1, one), (3, three)):
-        found += [(-place, (ref, 0), (ref, 32)), (place, (ref, 64), (ref, 96))]
+        found += [(place, (ref, 0), (ref, 32)), (-place, (ref, 64), (ref, 96))]
     found.append((4, (four, 0), (four, 32)))
 
     def target(place, part):

time: 70 us -> 70.3 us (level)
  blocking collectives: 15.5 us -> 17.4 us
  starting transfers between devices: 35.8 us -> 35 us
    all_gather x5, blocking collectives: 15.5 us -> 17.4 us  [both_cores(): return lax.all_gather(a, 'core', axis=0, tiled=True)]
    ppermute x5, starting transfers between devices: 19.6 us -> 18.7 us  [along(): return lax.ppermute(a, ('y', 'x_hi', 'core'), pairs)]
    ppermute x5, waiting for transfers between devices: 4.71 us -> 3.98 us  [along(): return lax.ppermute(a, ('y', 'x_hi', 'core'), pairs)]
  transfers between devices with their start and end apart: 7 -> 7, of which waited for: 3 -> 2; matrix products, arithmetic and copies ran while one was open for 0% -> 0% of each run, Pallas kernels for 0% -> 0%
where the time goes in v4:
time: 70.3 us; the launch traced here: 69.9 us
  starting transfers between devices  35 us (50%)
  blocking collectives  17.4 us (25%)
  waiting for transfers between devices  10.3 us (15%)
  Pallas kernels  4.43 us (6%)
  local copies, waits for them, and re-layouts  1.88 us (3%)
  between operations  0.75 us (1%)
    ppermute x5, starting transfers between devices, along(): return lax.ppermute(a, ('y', 'x_hi', 'core'), pairs)  18.7 us
    all_gather x5, blocking collectives, both_cores(): return lax.all_gather(a, 'core', axis=0, tiled=True)  17.4 us
    all_to_all x1, starting transfers between devices, per_device(): got = lax.all_to_all(sent, 'tensor', 0, 0).reshape(HALF, rows).T  11.9 us
    all_to_all x1, waiting for transfers between devices, per_device(): got = lax.all_to_all(sent, 'tensor', 0, 0).reshape(HALF, rows).T  6.27 us
    ppermute x1, starting transfers between devices, swap(): return lax.ppermute(a, axis, [(0, 1), (1, 0)])  4.35 us
    ppermute x5, waiting for transfers between devices, along(): return lax.ppermute(a, ('y', 'x_hi', 'core'), pairs)  3.98 us
    pallas_call x1, Pallas kernels, per_device(): kernel_of(export, (brief(512, cols), full(4, n_blocks), full(HALF, cols))...  3.7 us
    unnamed x5, local copies, waits for them, and re-layouts  1.62 us
  transfers between devices with their start and end apart: 7, of which 2 were waited for; matrix products, arithmetic and copies ran while one was open for 0% of the time, Pallas kernels for 0%

profile of v4, /device:TPU:1, one launch (start us, length us, event | category | flops | bytes accessed | tf_op | source)
XLA Modules:
  0.0 69.9 jit_solution(15698506961204115673)
XLA Ops:
  0.6 0.0 copy-start.1
  0.6 0.7 copy-done.1
  1.3 0.6 spread.1
  1.9 11.9 %all-to-all-start = ((bf16[16,4,16]{2,1,0:T(4,128)(2,1)}), bf16[16,4,16]{2,1,0:T(4,128)(2,1)S(1)}, u32[]{:S(2)}, u32[]{:S(2)}) async-start(bf16[16,4,16]{2,1,0:T(4,128)(2,1)} %spread.1), calls=%async_computation | async-start | bytes 32768 | tf_op jit(solution)/shard_map/all_to_all | solution.py:163
  13.8 0.0 copy-start
  13.8 0.9 %copy-done = f32[16,3328]{1,0:T(8,128)S(1)} copy-done((f32[16,3328]{1,0:T(8,128)S(1)}, f32[16,3328]{1,0:T(8,128)}, u32[]{:S(2)}) %copy-start) | copy-done | bytes 213016
  14.8 0.1 prepare.1
  14.9 6.3 %all-to-all-done = bf16[16,4,16]{2,1,0:T(4,128)(2,1)S(1)} async-done(((bf16[16,4,16]{2,1,0:T(4,128)(2,1)}), bf16[16,4,16]{2,1,0:T(4,128)(2,1)S(1)}, u32[]{:S(2)}, u32[]{:S(2)}) %all-to-all-start) | async-done | bytes 2080 | tf_op jit(solution)/shard_map/all_to_all | solution.py:163
  21.2 0.1 copy.6
  21.2 0.2 dynamic_update_slice.3
  21.4 3.7 %all_gather.15.a = bf16[32,3456]{1,0:T(8,128)(2,1)S(1)} all-gather(bf16[16,3456]{1,0:T(8,128)(2,1)S(1)} %dynamic_update_slice.3), channel_id=1, replica_groups=mesh['y'=8,'x_hi'=2,'core'=2,'tensor'=16] {'core'}, dimensions={0}, use_global_device_ids=true | all-gather | bytes 331776 | tf_op jit(solution)/shard_map/all_gather | solution.py:28
  25.1 4.3 %collective-permute-start = (bf16[32,3456]{1,0:T(8,128)(2,1)S(1)}, bf16[32,3456]{1,0:T(8,128)(2,1)S(1)}, u32[]{:S(2)}, u32[]{:S(2)}) collective-permute-start(bf16[32,3456]{1,0:T(8,128)(2,1)S(1)} %all_gather.15.a), channel_id=1, source_target_pairs={{0,32},{32,0},{1,33},{33,1},{2,34},{34,2},{3,35},{35,3},{4,36},{36... | collective-permute-start | bytes 663560 | tf_op jit(solution)/shard_map/ppermute | solution.py:32
  29.5 0.1 pad_add_fusion.at_ref
  29.6 4.4 %collective-permute-start.2 = (bf16[32,3456]{1,0:T(8,128)(2,1)S(1)}, bf16[32,3456]{1,0:T(8,128)(2,1)S(1)}, u32[]{:S(2)}, u32[]{:S(2)}) collective-permute-start(bf16[32,3456]{1,0:T(8,128)(2,1)S(1)} %all_gather.15.a), channel_id=1, source_target_pairs={{0,416},{16,176},{32,384},{48,144},{64,480},{80,240},{96,448},{112... | collective-permute-start | bytes 663560 | tf_op jit(solution)/shard_map/ppermute | solution.py:24
  34.0 5.4 %collective-permute-start.1 = (bf16[32,3456]{1,0:T(8,128)(2,1)S(1)}, bf16[32,3456]{1,0:T(8,128)(2,1)S(1)}, u32[]{:S(2)}, u32[]{:S(2)}) collective-permute-start(bf16[32,3456]{1,0:T(8,128)(2,1)S(1)} %all_gather.15.a), channel_id=1, source_target_pairs={{0,384},{16,144},{32,416},{48,176},{64,448},{80,208},{96,480},{112... | collective-permute-start | bytes 663560 | tf_op jit(solution)/shard_map/ppermute | solution.py:24
  39.5 0.0 collective-permute-done.b
  39.5 2.3 %collective-permute-start.3 = (bf16[64,3456]{1,0:T(8,128)(2,1)S(1)}, bf16[64,3456]{1,0:T(8,128)(2,1)S(1)}, u32[]{:S(2)}, u32[]{:S(2)}) collective-permute-start(bf16[64,3456]{1,0:T(8,128)(2,1)S(1)} %pad_maximum_fusion), channel_id=1, source_target_pairs={{0,448},{16,80},{32,480},{48,112},{64,0},{80,144},{96,32},{112,176... | collective-permute-start | bytes 1327112 | tf_op jit(solution)/shard_map/ppermute | solution.py:24
  41.8 4.0 %collective-permute-done.1 = bf16[32,3456]{1,0:T(8,128)(2,1)S(1)} collective-permute-done((bf16[32,3456]{1,0:T(8,128)(2,1)S(1)}, bf16[32,3456]{1,0:T(8,128)(2,1)S(1)}, u32[]{:S(2)}, u32[]{:S(2)}) %collective-permute-start.1) | collective-permute-done | bytes 221216 | tf_op jit(solution)/shard_map/ppermute | solution.py:24
  45.8 0.0 collective-permute-done.2
  45.8 0.1 broadcast_select_fusion
  45.9 4.5 %collective-permute-start.5 = (bf16[32,3456]{1,0:T(8,128)(2,1)S(1)}, bf16[32,3456]{1,0:T(8,128)(2,1)S(1)}, u32[]{:S(2)}, u32[]{:S(2)}) collective-permute-start(bf16[32,3456]{1,0:T(8,128)(2,1)S(1)} %get-tuple-element.9), channel_id=1, source_target_pairs={{0,384},{16,144},{32,416},{48,176},{64,448},{80,208},{96,480},{112... | collective-permute-start | bytes 663560 | tf_op jit(solution)/shard_map/ppermute | solution.py:24
  50.5 2.0 %collective-permute-start.4 = (bf16[64,3456]{1,0:T(8,128)(2,1)S(1)}, bf16[64,3456]{1,0:T(8,128)(2,1)S(1)}, u32[]{:S(2)}, u32[]{:S(2)}) collective-permute-start(bf16[64,3456]{1,0:T(8,128)(2,1)S(1)} %get-tuple-element.6), channel_id=1, source_target_pairs={{0,448},{16,80},{32,480},{48,112},{64,0},{80,144},{96,32},{112,176... | collective-permute-start | bytes 1327112 | tf_op jit(solution)/shard_map/ppermute | solution.py:24
  52.5 0.0 collective-permute-done.3
  52.5 5.4 %all_gather.16.two = bf16[128,3456]{1,0:T(8,128)(2,1)S(1)} all-gather(bf16[64,3456]{1,0:T(8,128)(2,1)S(1)} %get-tuple-element.6), channel_id=1, replica_groups=mesh['y'=8,'x_hi'=2,'core'=2,'tensor'=16] {'core'}, dimensions={0}, use_global_device_ids=true | all-gather | bytes 1327104 | tf_op jit(solution)/shard_map/all_gather | solution.py:28
  57.9 2.4 %all_gather.17.one = bf16[128,3456]{1,0:T(8,128)(2,1)S(1)} all-gather(bf16[64,3456]{1,0:T(8,128)(2,1)S(1)} %collective-permute-done.3), channel_id=1, replica_groups=mesh['y'=8,'x_hi'=2,'core'=2,'tensor'=16] {'core'}, dimensions={0}, use_global_device_ids=true | all-gather | bytes 1327104 | tf_op jit(solution)/shard_map/all_gather | solution.py:28
  60.3 0.0 collective-permute-done.5
  60.3 2.1 %all_gather.18.four = bf16[64,3456]{1,0:T(8,128)(2,1)S(1)} all-gather(bf16[32,3456]{1,0:T(8,128)(2,1)S(1)} %collective-permute-done.5), channel_id=1, replica_groups=mesh['y'=8,'x_hi'=2,'core'=2,'tensor'=16] {'core'}, dimensions={0}, use_global_device_ids=true | all-gather | bytes 663552 | tf_op jit(solution)/shard_map/all_gather | solution.py:28
  62.4 0.0 collective-permute-done.4
  62.4 3.8 %all_gather.19.three = bf16[128,3456]{1,0:T(8,128)(2,1)S(1)} all-gather(bf16[64,3456]{1,0:T(8,128)(2,1)S(1)} %collective-permute-done.4), channel_id=1, replica_groups=mesh['y'=8,'x_hi'=2,'core'=2,'tensor'=16] {'core'}, dimensions={0}, use_global_device_ids=true | all-gather | bytes 1327104 | tf_op jit(solution)/shard_map/all_gather | solution.py:28
  66.2 3.7 %export.1 = (bf16[512,3328]{1,0:T(8,128)(2,1)}, f32[4,26]{1,0:T(4,128)}, f32[64,3328]{1,0:T(8,128)}) custom-call(s32[3]{0:T(128)S(1)} %pad_add_fusion.at_ref, bf16[32,3456]{1,0:T(8,128)(2,1)S(1)} %all_gather.15.a, bf16[32,3456]{1,0:T(8,128)(2,1)S(1)} %collective-permute-done.b, bf16[128,3456]{1,0:T(8,128)(2,1)S(1)} %all_gather.16.two, ...), custom_call_target="tpu_custom_call" | custom-call | tf_op jit(solution)/shard_map/export/pallas_call | solution.py:177
  (2 shorter events, 0.1 us)
Async XLA Ops:
  0.6 0.7 copy-start.1
  1.9 19.2 %all-to-all-start = ((bf16[16,4,16]{2,1,0:T(4,128)(2,1)}), bf16[16,4,16]{2,1,0:T(4,128)(2,1)S(1)}, u32[]{:S(2)}, u32[]{:S(2)}) async-start(bf16[16,4,16]{2,1,0:T(4,128)(2,1)} %spread.1), calls=%async_computation | async-start | bytes 32768 | tf_op jit(solution)/shard_map/all_to_all | solution.py:163
  13.8 0.9 %copy-start = (f32[16,3328]{1,0:T(8,128)S(1)}, f32[16,3328]{1,0:T(8,128)}, u32[]{:S(2)}) copy-start(f32[16,3328]{1,0:T(8,128)} %m_ref.1) | copy-start | bytes 638980
  25.1 14.3 %collective-permute-start = (bf16[32,3456]{1,0:T(8,128)(2,1)S(1)}, bf16[32,3456]{1,0:T(8,128)(2,1)S(1)}, u32[]{:S(2)}, u32[]{:S(2)}) collective-permute-start(bf16[32,3456]{1,0:T(8,128)(2,1)S(1)} %all_gather.15.a), channel_id=1, source_target_pairs={{0,32},{32,0},{1,33},{33,1},{2,34},{34,2},{3,35},{35,3},{4,36},{36... | collective-permute-start | bytes 663560 | tf_op jit(solution)/shard_map/ppermute | solution.py:32
  29.6 16.2 %collective-permute-start.2 = (bf16[32,3456]{1,0:T(8,128)(2,1)S(1)}, bf16[32,3456]{1,0:T(8,128)(2,1)S(1)}, u32[]{:S(2)}, u32[]{:S(2)}) collective-permute-start(bf16[32,3456]{1,0:T(8,128)(2,1)S(1)} %all_gather.15.a), channel_id=1, source_target_pairs={{0,416},{16,176},{32,384},{48,144},{64,480},{80,240},{96,448},{112... | collective-permute-start | bytes 663560 | tf_op jit(solution)/shard_map/ppermute | solution.py:24
  34.0 11.8 %collective-permute-start.1 = (bf16[32,3456]{1,0:T(8,128)(2,1)S(1)}, bf16[32,3456]{1,0:T(8,128)(2,1)S(1)}, u32[]{:S(2)}, u32[]{:S(2)}) collective-permute-start(bf16[32,3456]{1,0:T(8,128)(2,1)S(1)} %all_gather.15.a), channel_id=1, source_target_pairs={{0,384},{16,144},{32,416},{48,176},{64,448},{80,208},{96,480},{112... | collective-permute-start | bytes 663560 | tf_op jit(solution)/shard_map/ppermute | solution.py:24
  39.5 12.9 %collective-permute-start.3 = (bf16[64,3456]{1,0:T(8,128)(2,1)S(1)}, bf16[64,3456]{1,0:T(8,128)(2,1)S(1)}, u32[]{:S(2)}, u32[]{:S(2)}) collective-permute-start(bf16[64,3456]{1,0:T(8,128)(2,1)S(1)} %pad_maximum_fusion), channel_id=1, source_target_pairs={{0,448},{16,80},{32,480},{48,112},{64,0},{80,144},{96,32},{112,176... | collective-permute-start | bytes 1327112 | tf_op jit(solution)/shard_map/ppermute | solution.py:24
  45.9 14.4 %collective-permute-start.5 = (bf16[32,3456]{1,0:T(8,128)(2,1)S(1)}, bf16[32,3456]{1,0:T(8,128)(2,1)S(1)}, u32[]{:S(2)}, u32[]{:S(2)}) collective-permute-start(bf16[32,3456]{1,0:T(8,128)(2,1)S(1)} %get-tuple-element.9), channel_id=1, source_target_pairs={{0,384},{16,144},{32,416},{48,176},{64,448},{80,208},{96,480},{112... | collective-permute-start | bytes 663560 | tf_op jit(solution)/shard_map/ppermute | solution.py:24
  50.5 12.0 %collective-permute-start.4 = (bf16[64,3456]{1,0:T(8,128)(2,1)S(1)}, bf16[64,3456]{1,0:T(8,128)(2,1)S(1)}, u32[]{:S(2)}, u32[]{:S(2)}) collective-permute-start(bf16[64,3456]{1,0:T(8,128)(2,1)S(1)} %get-tuple-element.6), channel_id=1, source_target_pairs={{0,448},{16,80},{32,480},{48,112},{64,0},{80,144},{96,32},{112,176... | collective-permute-start | bytes 1327112 | tf_op jit(solution)/shard_map/ppermute | solution.py:24
